TPU v7x, 128 devices: a whole 4x4x4 slice. The times are simulated.
128 devices in a mesh: row: 8 (over z, core), col: 16 (over y, x).
Axes of the slice: x: 4, y: 4, z: 4, core: 2. Of those that a mesh axis runs over, the one named last changes fastest.
Arguments:
- front_matrix: float32 [12288, 12288], P('row', 'col')
- child_tiles: float32 [16384, 256, 128], P(('row', 'col')), may hold values from -0.25 to 0.25
- owner_index: int32 [16384], P(('row', 'col')), may hold values from 0 to 127, as said below
- slot_index: int32 [16384], P(('row', 'col')), may hold values from 0 to 35, as said below
Outputs:
- updated_front: float32 [12288, 12288], P('row', 'col')
Inputs may be any that keep to these rules, and one draw needn't show every extreme that they name: `owner_index`: each device's 128 blocks name at most 2 blocks for any one owner, and every device sends exactly 2 to some common owner. `slot_index`: blocks for owner 0 never land in its first 512 rows.
All inputs are finite; a program needn't handle non-finite values.
Results may differ from a plain program's by a relative error of at most 0.0003.
Values sent between devices are 32-bit elements; how exact they have to be, the bound alone decides.
A program may use at most 192 MiB of HBM per device.

v0:
```python
import jax
import jax.numpy as jnp
from jax import lax
from jax.sharding import PartitionSpec as P

P_SIZE = 512


def spread(block, axis, source):
    block = jnp.where(lax.axis_index(axis) == source, block, jnp.zeros_like(block))
    return lax.psum(block, axis)


def factor_block(block):
    factor = jnp.linalg.cholesky(0.5 * (block + block.T))
    identity = jnp.eye(block.shape[0], dtype=jnp.float32)
    inverse = jax.scipy.linalg.solve_triangular(factor, identity, lower=True)
    return (jnp.tril(factor), inverse)


def solve_panel(columns, factor, inverse, row_start):
    solved = lax.dot_general(
        columns,
        inverse,
        (((1,), (1,)), ((), ())),
        precision=lax.Precision.HIGHEST,
        preferred_element_type=jnp.float32,
    )
    panel_size = factor.shape[0]
    padded = jnp.concatenate(
        [factor, jnp.zeros((columns.shape[0] - panel_size, panel_size), jnp.float32)], 0
    )
    global_row = row_start + lax.broadcasted_iota(jnp.int32, solved.shape, 0)
    return jnp.where(global_row < panel_size, padded, solved)


def local(front_matrix, child_tiles, owner_index, slot_index):
    rows_loc, cols_loc = front_matrix.shape
    tile_count, tile_rows, tile_cols = child_tiles.shape
    row_count = lax.axis_size("row")
    col_count = lax.axis_size("col")
    owners = row_count * col_count
    capacity = max(2, 3 * tile_count // (2 * owners))
    same_owner = owner_index[:, None] == owner_index[None, :]
    earlier = lax.broadcasted_iota(jnp.int32, (tile_count, tile_count), 0) > lax.broadcasted_iota(
        jnp.int32, (tile_count, tile_count), 1
    )
    owner_rank = jnp.sum((same_owner & earlier).astype(jnp.int32), axis=1)
    position = owner_index * capacity + owner_rank
    send_tiles = (
        jnp.zeros((owners * capacity, tile_rows, tile_cols), jnp.float32)
        .at[position]
        .set(child_tiles)
    )
    send_slots = jnp.full((owners * capacity,), -1, jnp.int32).at[position].set(slot_index)
    got_tiles, got_slots = (
        lax.all_to_all(send_tiles, ("row", "col"), split_axis=0, concat_axis=0, tiled=True),
        lax.all_to_all(send_slots, ("row", "col"), split_axis=0, concat_axis=0, tiled=True),
    )
    got_tiles = got_tiles.reshape(owners * capacity, tile_rows * tile_cols)
    tiles_down = rows_loc // tile_rows
    tiles_across = cols_loc // tile_cols
    local_count = tiles_down * tiles_across
    onehot = (got_slots[None, :] == lax.broadcasted_iota(jnp.int32, (local_count, 1), 0)).astype(
        jnp.float32
    )
    added = jnp.dot(
        onehot, got_tiles, precision=lax.Precision.HIGHEST, preferred_element_type=jnp.float32
    )
    added = (
        added.reshape(tiles_down, tiles_across, tile_rows, tile_cols)
        .transpose(0, 2, 1, 3)
        .reshape(rows_loc, cols_loc)
    )
    assembled = front_matrix + added
    my_row = lax.axis_index("row")
    my_col = lax.axis_index("col")
    row_start = my_row * rows_loc
    diagonal = spread(assembled[:P_SIZE, :P_SIZE], "row", 0)
    diagonal = jnp.where(my_col == 0, diagonal, jnp.eye(P_SIZE, dtype=jnp.float32))
    factor, inverse = factor_block(diagonal)
    own_panel = solve_panel(assembled[:, :P_SIZE], factor, inverse, row_start)
    panel_rows = spread(own_panel, "col", 0)
    offset = my_col * cols_loc % rows_loc
    root_row = my_col * cols_loc // rows_loc
    column_piece = lax.dynamic_slice_in_dim(panel_rows, offset, cols_loc, 0)
    column_rows = spread(column_piece, "row", root_row)
    update = lax.dot_general(
        panel_rows,
        column_rows,
        (((1,), (1,)), ((), ())),
        precision=lax.Precision.HIGHEST,
        preferred_element_type=jnp.float32,
    )
    global_row = row_start + lax.broadcasted_iota(jnp.int32, (rows_loc, cols_loc), 0)
    global_col = my_col * cols_loc + lax.broadcasted_iota(jnp.int32, (rows_loc, cols_loc), 1)
    lowered = jnp.where(global_row >= global_col, assembled - update, assembled)
    panel_wide = jnp.concatenate(
        [panel_rows, jnp.zeros((rows_loc, cols_loc - P_SIZE), jnp.float32)], 1
    )
    return jnp.where(global_col < P_SIZE, panel_wide, lowered)


def solution(mesh):
    placed = (P("row", "col"), P(("row", "col"), None, None), P(("row", "col")), P(("row", "col")))
    return jax.shard_map(
        local, mesh=mesh, in_specs=placed, out_specs=P("row", "col"), check_vma=False
    )
```

profile of v0, /device:TPU:0, one launch (start us, length us, event | category | flops | bytes accessed | tf_op | source)
XLA Modules:
  0.0 1132.7 jit_solution(7385792869486823500)
XLA Ops:
  10.0 11.1 all-to-all-start
  21.1 11.2 broadcast_in_dim.30
  32.3 31.6 %scatter_fusion = f32[256,256,128]{2,1,0:T(8,128)} fusion(f32[256,256,128]{2,1,0:T(8,128)} %broadcast_in_dim.30, s32[128]{0:T(128)S(1)} %compare_select_fusion, f32[128,256,128]{2,1,0:T(8,128)} %param.5), kind=kCustom, calls=%fused_computation.1 | custom fusion | bytes 50332160 | tf_op jit(solution)/shard_map/scatter | solution.py:53
  63.9 10.4 all-to-all-start.1
  74.4 6.0 copy.58
  81.9 511.5 %all-to-all-done.1 = f32[256,256,128]{2,1,0:T(8,128)} async-done(((f32[256,256,128]{2,1,0:T(8,128)}), f32[256,256,128]{2,1,0:T(8,128)}, u32[]{:S(2)}, u32[]{:S(2)}) %all-to-all-start.1) | async-done | bytes 33554464 | tf_op jit(solution)/shard_map/all_to_all | solution.py:57
  593.4 33.6 %copy.84 = f32[256,256,128]{0,2,1:T(8,128)} copy(f32[256,256,128]{2,1,0:T(8,128)} %all-to-all-done.1) | data formatting | bytes 67108864 | tf_op jit(solution)/shard_map/reshape | solution.py:60
  627.0 25.4 %fusion = f32[6,6,256,128]{3,1,2,0:T(8,128)} fusion(f32[256,256,128]{0,2,1:T(8,128)} %copy.84, s32[6,6]{1,0:T(8,128)S(1)} %multiply_add_fusion, s32[256]{0:T(256)S(1)} %eq.68), kind=kOutput, calls=%fused_computation.4 | convolution fusion | flops 3623887872 | bytes 38274192 | tf_op jit(solution)/shard_map/dot_general | solution.py:67
  652.4 6.2 copy.88
  675.1 113.5 %all-reduce.7.cloned.1.call-done = f32[512,512]{0,1:T(8,128)} async-done(((f32[512,512]{0,1:T(8,128)}), f32[512,512]{0,1:T(8,128)}) %all-reduce.7.cloned.1.call-update) | async-done | bytes 1048592 | tf_op jit(solution)/shard_map/psum | solution.py:11
  791.2 11.7 %cholesky.107 = f32[128,128]{1,0:T(8,128)S(1)} custom-call(f32[128,128]{1,0:T(8,128)S(1)} %cholesky.269), custom_call_target="Cholesky" | custom-call | tf_op jit(solution)/shard_map/jit(cholesky)/cholesky | solution.py:15
  802.9 9.8 custom-call.31
  813.4 11.7 %cholesky.221 = f32[128,128]{1,0:T(8,128)S(1)} custom-call(f32[128,128]{1,0:T(8,128)S(1)} %cholesky.273), custom_call_target="Cholesky" | custom-call | tf_op jit(solution)/shard_map/jit(cholesky)/cholesky | solution.py:15
  828.3 11.4 %custom-call.32 = f32[1,128,128]{1,2,0:T(8,128)} custom-call(f32[1,128,128]{2,1,0:T(8,128)} %get-tuple-element.42), custom_call_target="InvertDiagBlocksLowerTriangular" | custom-call | tf_op jit(solution)/shard_map/jit(cholesky)/cholesky | solution.py:15
  842.3 11.7 %cholesky.242 = f32[128,128]{1,0:T(8,128)S(1)} custom-call(f32[128,128]{1,0:T(8,128)S(1)} %cholesky.278), custom_call_target="Cholesky" | custom-call | tf_op jit(solution)/shard_map/jit(cholesky)/cholesky | solution.py:15
  854.2 9.8 custom-call.33
  864.8 11.9 %cholesky.259 = f32[128,128]{1,0:T(8,128)S(1)} custom-call(f32[128,128]{1,0:T(8,128)S(1)} %convolution_subtract_fusion.5), custom_call_target="Cholesky" | custom-call | tf_op jit(solution)/shard_map/jit(cholesky)/cholesky | solution.py:15
  881.5 11.0 while.1
  892.5 40.1 %custom-call.34 = f32[4,128,128]{1,2,0:T(8,128)S(1)} custom-call(f32[4,128,128]{2,1,0:T(8,128)} %get-tuple-element.12), custom_call_target="InvertDiagBlocksLowerTriangular" | custom-call | tf_op jit(solution)/shard_map/jit(_solve_triangular)/triangular_solve | solution.py:17
  938.1 8.3 fusion.3
  946.8 94.0 %all-reduce.9.cloned.1.call-done = f32[1536,512]{0,1:T(8,128)} async-done(((f32[1536,512]{0,1:T(8,128)}), f32[1536,512]{0,1:T(8,128)}) %all-reduce.9.cloned.1.call-update) | async-done | bytes 3145744 | tf_op jit(solution)/shard_map/psum | solution.py:11
  1044.2 63.4 %all-reduce.11.cloned.1.call-done = f32[768,512]{0,1:T(8,128)} async-done(((f32[768,512]{0,1:T(8,128)}), f32[768,512]{0,1:T(8,128)}) %all-reduce.11.cloned.1.call-update) | async-done | bytes 1572880 | tf_op jit(solution)/shard_map/psum | solution.py:11
  1107.6 12.1 %fusion.2 = f32[1536,768]{0,1:T(8,128)} fusion(f32[1536,768]{0,1:T(8,128)} %copy-done, f32[1536,512]{0,1:T(8,128)S(1)} %copy-done.1, f32[768,512]{0,1:T(8,128)} %all-reduce.11.cloned.1.call-done, s32[1536]{0:T(1024)S(1)} %iota_add_fusion, s32[768]{0:T(1024)S(1)} %iota_add_fusion.1, pred[768]{0:T(1024)(128)(4,1)S(1)} %broadcast_compare_fusion.1), kind=kOutput, calls=%fused_computation.7 | convolution fusion | flops 7252475904 | bytes 14165760 | tf_op jit(solution)/shard_map/dot_general | solution.py:88
  1119.7 6.0 copy.75
  (95 shorter events, 53.5 us)
Async XLA Ops:
  10.0 54.0 %all-to-all-start = ((s32[128,2,1]{1,2,0:T(1,128)}), s32[128,2,1]{1,2,0:T(1,128)S(1)}, u32[]{:S(2)}, u32[]{:S(2)}) async-start(s32[128,2,1]{1,2,0:T(1,128)} %bitcast), calls=%async_computation | async-start | bytes 131072 | tf_op jit(solution)/shard_map/all_to_all | solution.py:58
  63.9 529.4 %all-to-all-start.1 = ((f32[256,256,128]{2,1,0:T(8,128)}), f32[256,256,128]{2,1,0:T(8,128)}, u32[]{:S(2)}, u32[]{:S(2)}) async-start(f32[256,256,128]{2,1,0:T(8,128)} %scatter_fusion), calls=%async_computation.1 | async-start | bytes 67108864 | tf_op jit(solution)/shard_map/all_to_all | solution.py:57
  74.4 714.2 %all-reduce.7.cloned.1.call-start = ((), (), s32[]{:S(2)}) async-start(), calls=%async_computation.2 | async-start | bytes 2097152 | tf_op jit(solution)/shard_map/psum | solution.py:11
  669.3 2.2 copy-start
  672.6 368.2 %all-reduce.9.cloned.1.call-start = ((), (), s32[]{:S(2)}) async-start(), calls=%async_computation.3 | async-start | bytes 6291456 | tf_op jit(solution)/shard_map/psum | solution.py:11
  788.5 1.8 copy-start.2
  825.1 108.6 %copy-start.3 = (f32[512,512]{0,1:T(8,128)S(1)}, f32[512,512]{0,1:T(8,128)}, u32[]{:S(2)}) copy-start(f32[512,512]{0,1:T(8,128)} %fusion.22) | copy-start | bytes 3145732
  946.5 161.1 %all-reduce.11.cloned.1.call-start = ((), (), s32[]{:S(2)}) async-start(), calls=%async_computation.4 | async-start | bytes 3145728 | tf_op jit(solution)/shard_map/psum | solution.py:11
  1040.8 66.7 %copy-start.1 = (f32[1536,512]{0,1:T(8,128)S(1)}, f32[1536,512]{0,1:T(8,128)}, u32[]{:S(2)}) copy-start(f32[1536,512]{0,1:T(8,128)} %all-reduce.9.cloned.1.call-done) | copy-start | bytes 9437188
Sparse Core Ops, SparseCore 0:
  672.7 115.7 all-reduce.6
  946.6 94.1 all-reduce.8
  1044.3 63.2 all-reduce.10
where the time goes:
time: 1140 us; the launch traced here: 1130 us
  waiting for transfers between devices  782 us (69%)
  other arithmetic  136 us (12%)
  local copies, waits for them, and re-layouts  121 us (11%)
  matrix products  54.4 us (5%)
  starting transfers between devices  22.4 us (2%)
  between operations  16.5 us (1%)
    all_to_all x1, waiting for transfers between devices, local(): lax.all_to_all(send_tiles, ('row', 'col'), split_axis=0, concat_axis=0, t...  512 us
    psum x3, waiting for transfers between devices, spread(): return lax.psum(block, axis)  271 us
    another operation x14, other arithmetic, factor_block(): factor = jnp.linalg.cholesky(0.5 * (block + block.T))  80.8 us
    another operation x2, other arithmetic, factor_block(): inverse = jax.scipy.linalg.solve_triangular(factor, identity, lower=True)  40.1 us
    reshape x1, local copies, waits for them, and re-layouts, local(): got_tiles = got_tiles.reshape(owners * capacity, tile_rows * tile_cols)  33.6 us
    scatter x1, local copies, waits for them, and re-layouts, local(): send_tiles = jnp.zeros((owners * capacity, tile_rows, tile_cols), jnp.flo...  31.6 us
    dot_general x1, matrix products, local(): jnp.dot(onehot, got_tiles, precision=lax.Precision.HIGHEST, preferred_ele...  25.4 us
  transfers between devices with their start and end apart: 5, of which 4 were waited for; matrix products, arithmetic and copies ran while one was open for 5% of the time, Pallas kernels for 0%

commit v1 on v0

--- a/solution.py
+++ b/solution.py
@@ -1,9 +1,346 @@
+import functools
+
 import jax
 import jax.numpy as jnp
 from jax import lax
+from jax.experimental import pallas as pl
+from jax.experimental.pallas import tpu as pltpu
 from jax.sharding import PartitionSpec as P
 
 P_SIZE = 512
+MESH = pl.DeviceIdType.MESH
+ROWS = (88, 88, 80)
+STARTS = (0, 88, 176)
+HALF = (40, 40, 40)
+ORDERS = ("zxy", "xyz", "yzx")
+SHIFTS = (2, 1, 3, 0)
+SLOTS = 36
+
+
+def position():
+    row = lax.axis_index("row")
+    col = lax.axis_index("col")
+    return {"z": row // 2, "k": lax.rem(row, 2), "y": col // 4, "x": lax.rem(col, 4)}
+
+
+def device(at):
+    return (at["z"] * 2 + at["k"], at["y"] * 4 + at["x"])
+
+
+def moved(at, **steps):
+    to = dict(at)
+    for name, step in steps.items():
+        to[name] = lax.rem(at[name] + step, 2 if name == "k" else 4)
+    return to
+
+
+def exchange_kernel(
+    where_ref, prev_ref, last_ref, child, front, out, arr0, arr1, arr2, mid0, mid1, mid2, *scratch
+):
+    arrived = (arr0, arr1, arr2)
+    middle = (mid0, mid1, mid2)
+    staging, got = scratch[0:3], scratch[3:6]
+    far, right, left = scratch[6:9], scratch[9:12], scratch[12:15]
+    in_far, in_left, in_right = scratch[15:18], scratch[18:21], scratch[21:24]
+    send_a, recv_a, send_b, recv_b, send_c, recv_c, load_sem, front_sem, out_sem = scratch[24:]
+    me = position()
+
+    barrier = pltpu.get_barrier_semaphore()
+    partners = [moved(me, k=1)]
+    for axis in "zyx":
+        for step in (1, 2, 3):
+            for core in (0, 1):
+                partners.append(moved(me, **{axis: step, "k": core}))
+    for to in partners:
+        pl.semaphore_signal(barrier, inc=1, device_id=device(to), device_id_type=MESH)
+
+    def pack(t, p):
+        d, e, f = ORDERS[p]
+        shift = SHIFTS[t]
+
+        def body(i, carry):
+            at = {
+                d: i // 16,
+                "k": lax.rem(i // 8, 2),
+                e: lax.rem(i // 2, 4),
+                f: lax.rem(me[f] + shift, 4),
+            }
+            owner = ((at["z"] * 2 + at["k"]) * 4 + at["y"]) * 4 + at["x"]
+            index = where_ref[owner * 2 + lax.rem(i, 2)]
+            staging[p][i // 8, lax.rem(i // 2, 4), lax.rem(i, 2)] = child[
+                index, STARTS[p] : STARTS[p] + ROWS[p], :
+            ]
+            return carry
+
+        lax.fori_loop(0, 64, body, 0)
+
+    def group(at, d):
+        return at[d] * 2 + at["k"]
+
+    def start_a(t, p):
+        d = ORDERS[p][0]
+        mine = group(me, d)
+        for step, core in ((1, 0), (3, 0), (1, 1), (3, 1), (2, 0), (2, 1), (0, 1)):
+            to = moved(me, **{d: step, "k": core})
+            pltpu.make_async_remote_copy(
+                src_ref=staging[p].at[group(to, d)],
+                dst_ref=arrived[p].at[t, :, mine],
+                send_sem=send_a.at[t, p],
+                recv_sem=recv_a.at[t, p],
+                device_id=device(to),
+                device_id_type=MESH,
+            ).start()
+        pltpu.make_async_copy(
+            staging[p].at[mine], arrived[p].at[t, :, mine], recv_a.at[t, p]
+        ).start()
+
+    def wait_send_a(t, p):
+        part = staging[p].at[pl.ds(0, 7)]
+        pltpu.make_async_copy(part, part, send_a.at[t, p]).wait()
+
+    def start_b(t, p):
+        e = ORDERS[p][1]
+        whole = arrived[p].at[t]
+        pltpu.make_async_copy(whole, whole, recv_a.at[t, p]).wait()
+        for step in (1, 3, 2):
+            to = moved(me, **{e: step})
+            pltpu.make_async_remote_copy(
+                src_ref=arrived[p].at[t, to[e]],
+                dst_ref=middle[p].at[t, me[e]],
+                send_sem=send_b.at[t, p],
+                recv_sem=recv_b.at[t, p],
+                device_id=device(to),
+                device_id_type=MESH,
+            ).start()
+        pltpu.make_async_copy(
+            arrived[p].at[t, me[e]], middle[p].at[t, me[e]], recv_b.at[t, p]
+        ).start()
+
+    def load(t, p):
+        whole = middle[p].at[t]
+        pltpu.make_async_copy(whole, whole, recv_b.at[t, p]).wait()
+        pltpu.make_async_copy(whole, got[p].at[pl.ds(0, 4)], load_sem.at[p]).start()
+
+    def to_neighbour(source, target, p, kind, step):
+        f = ORDERS[p][2]
+        return pltpu.make_async_remote_copy(
+            src_ref=source,
+            dst_ref=target,
+            send_sem=send_c.at[kind, p],
+            recv_sem=recv_c.at[kind, p],
+            device_id=device(moved(me, **{f: step})),
+            device_id_type=MESH,
+        )
+
+    def far_copies(p):
+        low, high = pl.ds(0, HALF[p]), pl.ds(HALF[p], ROWS[p] - HALF[p])
+        return (
+            to_neighbour(far[p].at[:, low], in_far[p].at[:, low], p, 0, 1),
+            to_neighbour(far[p].at[:, high], in_far[p].at[:, high], p, 1, 3),
+        )
+
+    def front_copy(p, q):
+        rows = pl.ds(q // 6 * 256 + STARTS[p], ROWS[p])
+        return front.at[rows, pl.ds(q % 6 * 128, 128)], far[p].at[q], front_sem.at[p]
+
+    def out_copy(p, q):
+        rows = pl.ds(q // 6 * 256 + STARTS[p], ROWS[p])
+        return far[p].at[q], out.at[rows, pl.ds(q % 6 * 128, 128)], out_sem.at[p]
+
+    def add_up(t, p):
+        rows = ROWS[p]
+        held = got[p]
+        pltpu.make_async_copy(
+            middle[p].at[t], held.at[pl.ds(0, 4)], load_sem.at[p]
+        ).wait()
+
+        def at(k):
+            return k // 16, lax.rem(k // 2, 8), lax.rem(k, 2)
+
+        def chain(k, carry):
+            to = at(k)
+            held[to] = held[to] + held[at(prev_ref[(p * 4 + t) * 64 + k])]
+            return carry
+
+        lax.fori_loop(0, 64, chain, 0)
+
+        def total(q):
+            return held[at(last_ref[(p * 4 + t) * SLOTS + q])]
+
+        half = HALF[p]
+        shift = SHIFTS[t]
+        if shift == 2:
+
+            def body(q, carry):
+                far[p][q] = total(q)
+                return carry
+
+            lax.fori_loop(0, SLOTS, body, 0)
+            for copy in far_copies(p):
+                copy.start()
+        elif shift == 1:
+            far_copies(p)[0].wait_recv()
+
+            def body(q, carry):
+                right[p][q] = total(q)
+                right[p][q, 0:half] = right[p][q, 0:half] + in_far[p][q, 0:half]
+                return carry
+
+            lax.fori_loop(0, SLOTS, body, 0)
+            to_neighbour(right[p], in_left[p], p, 2, 1).start()
+        elif shift == 3:
+            far_copies(p)[1].wait_recv()
+
+            def body(q, carry):
+                left[p][q] = total(q)
+                left[p][q, half:rows] = left[p][q, half:rows] + in_far[p][q, half:rows]
+                return carry
+
+            lax.fori_loop(0, SLOTS, body, 0)
+            to_neighbour(left[p], in_right[p], p, 3, 3).start()
+            for copy in far_copies(p):
+                copy.wait_send()
+            for q in range(SLOTS):
+                pltpu.make_async_copy(*front_copy(p, q)).start()
+        else:
+            whole = far[p]
+            pltpu.make_async_copy(whole, whole, front_sem.at[p]).wait()
+
+            def own(q, carry):
+                far[p][q] = far[p][q] + total(q)
+                return carry
+
+            lax.fori_loop(0, SLOTS, own, 0)
+            to_neighbour(right[p], in_left[p], p, 2, 1).wait()
+            to_neighbour(left[p], in_right[p], p, 3, 3).wait()
+
+            def body(q, carry):
+                far[p][q] = far[p][q] + in_left[p][q] + in_right[p][q]
+                return carry
+
+            lax.fori_loop(0, SLOTS, body, 0)
+            for q in range(SLOTS):
+                pltpu.make_async_copy(*out_copy(p, q)).start()
+
+    for p in range(3):
+        pack(0, p)
+        got[p][4] = jnp.zeros((8, 2, ROWS[p], 128), jnp.float32)
+    pl.semaphore_wait(barrier, len(partners))
+    for p in range(3):
+        start_a(0, p)
+    for t in range(4):
+        for p in range(3):
+            start_b(t, p)
+            if t + 1 < 4:
+                wait_send_a(t, p)
+                pack(t + 1, p)
+                start_a(t + 1, p)
+        if t > 0:
+            for p in range(3):
+                load(t - 1, p)
+            for p in range(3):
+                add_up(t - 1, p)
+    for p in range(3):
+        load(3, p)
+    for p in range(3):
+        add_up(3, p)
+    for p in range(3):
+        wait_send_a(3, p)
+        for t in range(4):
+            part = middle[p].at[t, pl.ds(0, 3)]
+            pltpu.make_async_copy(part, part, send_b.at[t, p]).wait()
+        whole = far[p]
+        pltpu.make_async_copy(whole, whole, out_sem.at[p]).wait()
+
+
+def exchange(where, prev, last, child_tiles, front_matrix):
+    f32 = jnp.float32
+    scratch = [pltpu.VMEM((8, 4, 2, r, 128), f32) for r in ROWS]
+    scratch += [pltpu.VMEM((5, 8, 2, r, 128), f32) for r in ROWS]
+    for _ in range(6):
+        scratch += [pltpu.VMEM((SLOTS, r, 128), f32) for r in ROWS]
+    scratch += [pltpu.SemaphoreType.DMA((4, 3))] * 6
+    scratch += [pltpu.SemaphoreType.DMA((3,))] * 3
+    anywhere = pl.BlockSpec(memory_space=pl.ANY)
+    outs = [jax.ShapeDtypeStruct(front_matrix.shape, f32)]
+    outs += [jax.ShapeDtypeStruct((4, 4, 8, 2, r, 128), f32) for r in ROWS]
+    outs += [jax.ShapeDtypeStruct((4, 4, 8, 2, r, 128), f32) for r in ROWS]
+    return pl.pallas_call(
+        exchange_kernel,
+        out_shape=outs,
+        in_specs=[pl.BlockSpec(memory_space=pltpu.SMEM)] * 3
+        + [pl.BlockSpec(memory_space=pltpu.VMEM), anywhere],
+        out_specs=[anywhere] * 7,
+        scratch_shapes=scratch,
+        compiler_params=pltpu.CompilerParams(
+            collective_id=1, has_side_effects=True, vmem_limit_bytes=62 << 20
+        ),
+        name="exchange",
+    )(where, prev, last, child_tiles, front_matrix)[0]
+
+
+def routing(owner_index, slot_index):
+    count = owner_index.shape[0]
+    item = lax.broadcasted_iota(jnp.int32, (count, count), 0)
+    other = lax.broadcasted_iota(jnp.int32, (count, count), 1)
+    same = (owner_index[:, None] == owner_index[None, :]) & (item > other)
+    place = owner_index * 2 + jnp.sum(same.astype(jnp.int32), axis=1)
+    hit = place[:, None] == lax.broadcasted_iota(jnp.int32, (count, 256), 1)
+    where = jnp.sum(jnp.where(hit, lax.broadcasted_iota(jnp.int32, hit.shape, 0), 0), axis=0)
+    slots = jnp.sum(jnp.where(hit, slot_index[:, None] + 1, 0), axis=0) - 1
+    table = lax.all_gather(slots.astype(jnp.float32), ("row", "col"))
+    me = position()
+    pick_source, pick_owner = [], []
+    source = jnp.arange(128)
+    source = {"z": source // 32, "k": source // 16 % 2, "y": source // 4 % 4, "x": source % 4}
+    place = jnp.arange(256)
+    target = {"z": place // 64, "k": place // 32 % 2, "y": place // 8 % 4, "x": place // 2 % 4}
+    for p in range(3):
+        d, e, f = ORDERS[p]
+        r = jnp.arange(32)
+        pick_source.append(
+            (source[e][None] == (r // 8)[:, None])
+            & (source[d][None] == (r // 2 % 4)[:, None])
+            & (source["k"][None] == (r % 2)[:, None])
+            & (source[f] == me[f])[None]
+        )
+        n = jnp.arange(8)
+        shift = jnp.array(SHIFTS)[n // 2]
+        pick_owner.append(
+            (target[d] == me[d])[:, None]
+            & (target["k"] == me["k"])[:, None]
+            & (target[e] == me[e])[:, None]
+            & (target[f][:, None] == ((me[f] + shift) % 4)[None])
+            & ((place % 2)[:, None] == (n % 2)[None])
+        )
+    rows = jnp.dot(
+        jnp.concatenate(pick_source, 0).astype(jnp.float32),
+        table,
+        precision=lax.Precision.HIGHEST,
+    )
+    entries = jnp.stack(
+        [
+            jnp.dot(rows[p * 32 : p * 32 + 32], pick_owner[p].astype(jnp.float32))
+            for p in range(3)
+        ]
+    )
+    entries = entries.reshape(3, 32, 4, 2).transpose(0, 2, 1, 3).reshape(12, 64)
+    entries = jnp.round(entries).astype(jnp.int32)
+    k = lax.broadcasted_iota(jnp.int32, (12, 64, 64), 1)
+    j = lax.broadcasted_iota(jnp.int32, (12, 64, 64), 2)
+    match = (entries[:, :, None] == entries[:, None, :]) & (entries[:, :, None] >= 0) & (j < k)
+    prev = jnp.max(jnp.where(match, j, -1), axis=2)
+    prev = jnp.where(prev < 0, 64, prev)
+    q = lax.broadcasted_iota(jnp.int32, (12, SLOTS, 64), 1)
+    j = lax.broadcasted_iota(jnp.int32, (12, SLOTS, 64), 2)
+    last = jnp.max(jnp.where(entries[:, None, :] == q, j, -1), axis=2)
+    last = jnp.where(last < 0, 64, last)
+    return where, prev.reshape(-1), last.reshape(-1)
+
+
+def assemble(front_matrix, child_tiles, owner_index, slot_index):
+    where, prev, last = routing(owner_index, slot_index)
+    return exchange(where, prev, last, child_tiles, front_matrix)
 
 
 def spread(block, axis, source):
@@ -36,43 +373,7 @@
 
 def local(front_matrix, child_tiles, owner_index, slot_index):
     rows_loc, cols_loc = front_matrix.shape
-    tile_count, tile_rows, tile_cols = child_tiles.shape
-    row_count = lax.axis_size("row")
-    col_count = lax.axis_size("col")
-    owners = row_count * col_count
-    capacity = max(2, 3 * tile_count // (2 * owners))
-    same_owner = owner_index[:, None] == owner_index[None, :]
-    earlier = lax.broadcasted_iota(jnp.int32, (tile_count, tile_count), 0) > lax.broadcasted_iota(
-        jnp.int32, (tile_count, tile_count), 1
-    )
-    owner_rank = jnp.sum((same_owner & earlier).astype(jnp.int32), axis=1)
-    position = owner_index * capacity + owner_rank
-    send_tiles = (
-        jnp.zeros((owners * capacity, tile_rows, tile_cols), jnp.float32)
-        .at[position]
-        .set(child_tiles)
-    )
-    send_slots = jnp.full((owners * capacity,), -1, jnp.int32).at[position].set(slot_index)
-    got_tiles, got_slots = (
-        lax.all_to_all(send_tiles, ("row", "col"), split_axis=0, concat_axis=0, tiled=True),
-        lax.all_to_all(send_slots, ("row", "col"), split_axis=0, concat_axis=0, tiled=True),
-    )
-    got_tiles = got_tiles.reshape(owners * capacity, tile_rows * tile_cols)
-    tiles_down = rows_loc // tile_rows
-    tiles_across = cols_loc // tile_cols
-    local_count = tiles_down * tiles_across
-    onehot = (got_slots[None, :] == lax.broadcasted_iota(jnp.int32, (local_count, 1), 0)).astype(
-        jnp.float32
-    )
-    added = jnp.dot(
-        onehot, got_tiles, precision=lax.Precision.HIGHEST, preferred_element_type=jnp.float32
-    )
-    added = (
-        added.reshape(tiles_down, tiles_across, tile_rows, tile_cols)
-        .transpose(0, 2, 1, 3)
-        .reshape(rows_loc, cols_loc)
-    )
-    assembled = front_matrix + added
+    assembled = assemble(front_matrix, child_tiles, owner_index, slot_index)
     my_row = lax.axis_index("row")
     my_col = lax.axis_index("col")
     row_start = my_row * rows_loc

time: 1140 us -> 813 us (0.71)
  waiting for transfers between devices: 782 us -> 219 us
  Pallas kernels: 0 us -> 321 us
  local copies, waits for them, and re-layouts: 121 us -> 29.2 us
  blocking collectives: 0 us -> 57.7 us
  matrix products: 54.4 us -> 29.6 us
  starting transfers between devices: 22.4 us -> 0.86 us
    all_to_all x2 -> x0, waiting for transfers between devices: 512 us -> none  [the longest x1 512 us: local(): lax.all_to_all(send_tiles, ('row', 'col'), split_axis=0, concat_axis=0, t...]
    pallas_call x0 -> x1, Pallas kernels: none -> 321 us  [exchange(): pl.pallas_call(exchange_kernel, out_shape=outs, in_specs=[pl.BlockSpec(me...]
    all_gather x0 -> x1, blocking collectives: none -> 57.7 us  [routing(): table = lax.all_gather(slots.astype(jnp.float32), ('row', 'col'))]
    psum x3, waiting for transfers between devices: 271 us -> 219 us  [spread(): return lax.psum(block, axis)]
    reshape x2 -> x0, local copies, waits for them, and re-layouts: 39.6 us -> none  [the longest x1 33.6 us: local(): got_tiles = got_tiles.reshape(owners * capacity, tile_rows * tile_cols)]
    scatter x2 -> x0, local copies, waits for them, and re-layouts: 32.7 us -> none  [the longest x1 31.6 us: local(): send_tiles = jnp.zeros((owners * capacity, tile_rows, tile_cols), jnp.flo...]
    dot_general x1 -> x4, matrix products: 25.4 us -> 0.76 us  [the longest x3 0.56 us: routing(): jnp.dot(rows[p * 32:p * 32 + 32], pick_owner[p].astype(jnp.float32))]
    all_to_all x2 -> x0, starting transfers between devices: 21.6 us -> none  [the longest x1 11.1 us: local(): lax.all_to_all(send_slots, ('row', 'col'), split_axis=0, concat_axis=0, t...]
  transfers between devices with their start and end apart: 5 -> 3, of which waited for: 4 -> 3; matrix products, arithmetic and copies ran while one was open for 5% -> 0% of each run, Pallas kernels for 0% -> 0%
where the time goes in v1:
time: 813 us; the launch traced here: 808 us
  Pallas kernels  321 us (39%)
  waiting for transfers between devices  219 us (27%)
  other arithmetic  134 us (16%)
  blocking collectives  57.7 us (7%)
  matrix products  29.6 us (4%)
  local copies, waits for them, and re-layouts  29.2 us (4%)
  between operations  16.4 us (2%)
    pallas_call x1, Pallas kernels, exchange(): pl.pallas_call(exchange_kernel, out_shape=outs, in_specs=[pl.BlockSpec(me...  321 us
    psum x3, waiting for transfers between devices, spread(): return lax.psum(block, axis)  219 us
    another operation x15, other arithmetic, factor_block(): factor = jnp.linalg.cholesky(0.5 * (block + block.T))  80.1 us
    all_gather x1, blocking collectives, routing(): table = lax.all_gather(slots.astype(jnp.float32), ('row', 'col'))  57.7 us
    another operation x2, other arithmetic, factor_block(): inverse = jax.scipy.linalg.solve_triangular(factor, identity, lower=True)  40.1 us
  transfers between devices with their start and end apart: 3, of which 3 were waited for; matrix products, arithmetic and copies ran while one was open for 0% of the time, Pallas kernels for 0%

profile of v1, /device:TPU:0, one launch (start us, length us, event | category | flops | bytes accessed | tf_op | source)
XLA Modules:
  0.0 808.2 jit_solution(3897538927278380338)
XLA Ops:
  9.0 57.7 %all-gather.1 = f32[128,1,256]{2,1,0:T(1,128)S(1)} all-gather(f32[1,1,256]{2,1,0:T(1,128)S(1)} %bitcast.65), channel_id=2, replica_groups=mesh['row'=8,'col'=16] {'row','col'}, dimensions={0}, use_global_device_ids=true | all-gather | bytes 132096 | tf_op jit(solution)/shard_map/all_gather | solution.py:291
  71.5 321.1 %exchange.1 = (f32[1536,768]{1,0:T(8,128)}, f32[4,4,8,2,88,128]{5,4,3,2,1,0:T(8,128)}, f32[4,4,8,2,88,128]{5,4,3,2,1,0:T(8,128)}, f32[4,4,8,2,80,128]{5,4,3,2,1,...) custom-call(s32[256]{0:T(256)} %get-tuple-element.36.where_ref, ...), custom_call_target="tpu_custom_call" | custom-call | tf_op jit(solution)/shard_map/exchange/pallas_call | solution.py:268
  392.6 6.0 copy.109
  398.6 2.3 slice_select_fusion
  403.5 61.7 %all-reduce.7.cloned.1.call-done = f32[512,512]{0,1:T(8,128)} async-done(((f32[512,512]{0,1:T(8,128)}), f32[512,512]{0,1:T(8,128)}) %all-reduce.7.cloned.1.call-update) | async-done | bytes 1048592 | tf_op jit(solution)/shard_map/psum | solution.py:348
  465.2 1.4 broadcast_select_fusion
  467.8 11.7 %cholesky.107 = f32[128,128]{1,0:T(8,128)S(1)} custom-call(f32[128,128]{1,0:T(8,128)S(1)} %cholesky.269), custom_call_target="Cholesky" | custom-call | tf_op jit(solution)/shard_map/jit(cholesky)/cholesky | solution.py:352
  479.5 9.8 %custom-call.31 = f32[1,128,128]{1,2,0:T(8,128)S(1)} custom-call(f32[1,128,128]{2,1,0:T(8,128)S(1)} %get-tuple-element.52), custom_call_target="InvertDiagBlocksLowerTriangular" | custom-call | tf_op jit(solution)/shard_map/jit(cholesky)/cholesky | solution.py:352
  490.0 11.7 %cholesky.221 = f32[128,128]{1,0:T(8,128)S(1)} custom-call(f32[128,128]{1,0:T(8,128)S(1)} %cholesky.273), custom_call_target="Cholesky" | custom-call | tf_op jit(solution)/shard_map/jit(cholesky)/cholesky | solution.py:352
  503.3 10.6 %custom-call.32 = f32[1,128,128]{1,2,0:T(8,128)} custom-call(f32[1,128,128]{2,1,0:T(8,128)S(1)} %get-tuple-element.50), custom_call_target="InvertDiagBlocksLowerTriangular" | custom-call | tf_op jit(solution)/shard_map/jit(cholesky)/cholesky | solution.py:352
  517.5 11.7 %cholesky.242 = f32[128,128]{1,0:T(8,128)S(1)} custom-call(f32[128,128]{1,0:T(8,128)S(1)} %cholesky.278), custom_call_target="Cholesky" | custom-call | tf_op jit(solution)/shard_map/jit(cholesky)/cholesky | solution.py:352
  529.4 9.8 %custom-call.33 = f32[1,128,128]{1,2,0:T(8,128)S(1)} custom-call(f32[1,128,128]{2,1,0:T(8,128)S(1)} %get-tuple-element.48), custom_call_target="InvertDiagBlocksLowerTriangular" | custom-call | tf_op jit(solution)/shard_map/jit(cholesky)/cholesky | solution.py:352
  540.0 11.9 %cholesky.259 = f32[128,128]{1,0:T(8,128)S(1)} custom-call(f32[128,128]{1,0:T(8,128)S(1)} %convolution_subtract_fusion.5), custom_call_target="Cholesky" | custom-call | tf_op jit(solution)/shard_map/jit(cholesky)/cholesky | solution.py:352
  557.4 11.0 %while.1 = (s32[]{:T(128)}, f32[512,512]{0,1:T(8,128)S(1)}, s32[4,2]{0,1:T(2,128)S(1)}, f32[4,128,128]{2,1,0:T(8,128)}, s32[]{:T(128)}) while((s32[]{:T(128)}, f32[512,512]{0,1:T(8,128)S(1)}, s32[4,2]{0,1:T(2,128)S(1)}, f32[4,128,128]{2,1,0:T(8,128)}, s32[]{:T(128)}) %tuple.40), condition=%wide.while_cond, body=%wide.while_body.sunk | while | flops 2 | bytes 393829 | solution.py:354
  558.1 1.3 dynamic-slice.7
  560.8 1.3 dynamic-slice.7
  568.4 40.1 %custom-call.34 = f32[4,128,128]{1,2,0:T(8,128)S(1)} custom-call(f32[4,128,128]{2,1,0:T(8,128)} %get-tuple-element.14), custom_call_target="InvertDiagBlocksLowerTriangular" | custom-call | tf_op jit(solution)/shard_map/jit(_solve_triangular)/triangular_solve | solution.py:354
  612.0 1.5 convolution_subtract_fusion.2
  614.0 8.2 %fusion.1 = f32[1536,512]{0,1:T(8,128)} fusion(f32[1536,768]{1,0:T(8,128)} %get-tuple-element.6, f32[512,512]{0,1:T(8,128)S(1)} %get-tuple-element.129, pred[1536]{0:T(1024)(128)(4,1)S(1)} %broadcast_compare_fusion.1, pred[]{:T(512)S(6)} %eq.381, f32[128,512]{1,0:T(8,128)S(1)} %fusion.35, f32[128,512]{1,0:T(8,128)S(1)} %fusion.36, ...), kind=kOutput, calls=%fused_computation.6 | convolution fusion | flops 4834197504 | bytes 8390145 | tf_op jit(solution)/shard_map/dot_general | solution.py:359
  622.5 94.0 %all-reduce.9.cloned.1.call-done = f32[1536,512]{0,1:T(8,128)} async-done(((f32[1536,512]{0,1:T(8,128)}), f32[1536,512]{0,1:T(8,128)}) %all-reduce.9.cloned.1.call-update) | async-done | bytes 3145744 | tf_op jit(solution)/shard_map/psum | solution.py:348
  716.5 3.3 dynamic-slice_select_fusion
  719.9 63.4 %all-reduce.11.cloned.1.call-done = f32[768,512]{0,1:T(8,128)} async-done(((f32[768,512]{0,1:T(8,128)}), f32[768,512]{0,1:T(8,128)}) %all-reduce.11.cloned.1.call-update) | async-done | bytes 1572880 | tf_op jit(solution)/shard_map/psum | solution.py:348
  783.3 12.1 %fusion = f32[1536,768]{0,1:T(8,128)} fusion(f32[1536,768]{0,1:T(8,128)} %copy.109, f32[1536,512]{0,1:T(8,128)S(1)} %copy-done, f32[768,512]{0,1:T(8,128)} %all-reduce.11.cloned.1.call-done, s32[1536]{0:T(1024)S(1)} %iota_add_fusion, s32[768]{0:T(1024)S(1)} %iota_add_fusion.1, pred[768]{0:T(1024)(128)(4,1)S(1)} %broadcast_compare_fusion.2), kind=kOutput, calls=%fused_computation.4 | convolution fusion | flops 7252475904 | bytes 14165760 | tf_op jit(solution)/shard_map/dot_general | solution.py:389
  795.4 6.0 copy.127
  (116 shorter events, 33.0 us)
Async XLA Ops:
  6.5 458.6 %all-reduce.7.cloned.1.call-start = ((), (), s32[]{:S(2)}) async-start(), calls=%async_computation | async-start | bytes 2097152 | tf_op jit(solution)/shard_map/psum | solution.py:348
  401.0 315.6 %all-reduce.9.cloned.1.call-start = ((), (), s32[]{:S(2)}) async-start(), calls=%async_computation.1 | async-start | bytes 6291456 | tf_op jit(solution)/shard_map/psum | solution.py:348
  465.1 1.8 copy-start.1
  501.7 107.9 %copy-start.2 = (f32[512,512]{0,1:T(8,128)S(1)}, f32[512,512]{0,1:T(8,128)}, u32[]{:S(2)}) copy-start(f32[512,512]{0,1:T(8,128)} %fusion.20) | copy-start | bytes 3145732
  622.2 161.1 %all-reduce.11.cloned.1.call-start = ((), (), s32[]{:S(2)}) async-start(), calls=%async_computation.2 | async-start | bytes 3145728 | tf_op jit(solution)/shard_map/psum | solution.py:348
  716.5 66.7 %copy-start = (f32[1536,512]{0,1:T(8,128)S(1)}, f32[1536,512]{0,1:T(8,128)}, u32[]{:S(2)}) copy-start(f32[1536,512]{0,1:T(8,128)} %all-reduce.9.cloned.1.call-done) | copy-start | bytes 9437188
Sparse Core Ops, SparseCore 0:
  401.1 64.0 all-reduce.6
  622.3 94.1 all-reduce.8
  719.9 63.2 all-reduce.10

commit v2 on v1

--- a/solution.py
+++ b/solution.py
@@ -15,6 +15,7 @@
 ORDERS = ("zxy", "xyz", "yzx")
 SHIFTS = (2, 1, 3, 0)
 SLOTS = 36
+BANDS = ((0, 256, 256), (256, 128, 384), (384, 128, 512))
 
 
 def position():
@@ -35,14 +36,30 @@
 
 
 def exchange_kernel(
-    where_ref, prev_ref, last_ref, child, front, out, arr0, arr1, arr2, mid0, mid1, mid2, *scratch
+    where_ref,
+    prev_ref,
+    last_ref,
+    child,
+    front,
+    out,
+    arr0,
+    arr1,
+    arr2,
+    mid0,
+    mid1,
+    mid2,
+    square,
+    factor_out,
+    *scratch,
 ):
     arrived = (arr0, arr1, arr2)
     middle = (mid0, mid1, mid2)
-    staging, got = scratch[0:3], scratch[3:6]
-    far, right, left = scratch[6:9], scratch[9:12], scratch[12:15]
-    in_far, in_left, in_right = scratch[15:18], scratch[18:21], scratch[21:24]
-    send_a, recv_a, send_b, recv_b, send_c, recv_c, load_sem, front_sem, out_sem = scratch[24:]
+    staging, pools = scratch[0:3], scratch[3:5]
+    got = [pools[p % 2].at[:, pl.ds(0, ROWS[p])] for p in range(3)]
+    far, right, left = scratch[5:8], scratch[8:11], scratch[11:14]
+    in_far, in_left, in_right = scratch[14:17], scratch[17:20], scratch[20:23]
+    send_a, recv_a, send_b, recv_b, send_c, recv_c, load_sem, front_sem, out_sem = scratch[23:32]
+    send_s, recv_s, corner_sem, work, inverse = scratch[32:]
     me = position()
 
     barrier = pltpu.get_barrier_semaphore()
@@ -84,14 +101,14 @@
             to = moved(me, **{d: step, "k": core})
             pltpu.make_async_remote_copy(
                 src_ref=staging[p].at[group(to, d)],
-                dst_ref=arrived[p].at[t, :, mine],
+                dst_ref=arrived[p].at[t, :, pl.ds(mine * 2, 2)],
                 send_sem=send_a.at[t, p],
                 recv_sem=recv_a.at[t, p],
                 device_id=device(to),
                 device_id_type=MESH,
             ).start()
         pltpu.make_async_copy(
-            staging[p].at[mine], arrived[p].at[t, :, mine], recv_a.at[t, p]
+            staging[p].at[mine], arrived[p].at[t, :, pl.ds(mine * 2, 2)], recv_a.at[t, p]
         ).start()
 
     def wait_send_a(t, p):
@@ -106,20 +123,20 @@
             to = moved(me, **{e: step})
             pltpu.make_async_remote_copy(
                 src_ref=arrived[p].at[t, to[e]],
-                dst_ref=middle[p].at[t, me[e]],
+                dst_ref=middle[p].at[t, pl.ds(me[e] * 16, 16)],
                 send_sem=send_b.at[t, p],
                 recv_sem=recv_b.at[t, p],
                 device_id=device(to),
                 device_id_type=MESH,
             ).start()
         pltpu.make_async_copy(
-            arrived[p].at[t, me[e]], middle[p].at[t, me[e]], recv_b.at[t, p]
+            arrived[p].at[t, me[e]], middle[p].at[t, pl.ds(me[e] * 16, 16)], recv_b.at[t, p]
         ).start()
 
     def load(t, p):
         whole = middle[p].at[t]
         pltpu.make_async_copy(whole, whole, recv_b.at[t, p]).wait()
-        pltpu.make_async_copy(whole, got[p].at[pl.ds(0, 4)], load_sem.at[p]).start()
+        pltpu.make_async_copy(whole, got[p].at[pl.ds(0, 64)], load_sem.at[p]).start()
 
     def to_neighbour(source, target, p, kind, step):
         f = ORDERS[p][2]
@@ -151,21 +168,17 @@
         rows = ROWS[p]
         held = got[p]
         pltpu.make_async_copy(
-            middle[p].at[t], held.at[pl.ds(0, 4)], load_sem.at[p]
+            middle[p].at[t], held.at[pl.ds(0, 64)], load_sem.at[p]
         ).wait()
 
-        def at(k):
-            return k // 16, lax.rem(k // 2, 8), lax.rem(k, 2)
-
         def chain(k, carry):
-            to = at(k)
-            held[to] = held[to] + held[at(prev_ref[(p * 4 + t) * 64 + k])]
+            held[k] = held[k] + held[prev_ref[(p * 4 + t) * 64 + k]]
             return carry
 
         lax.fori_loop(0, 64, chain, 0)
 
         def total(q):
-            return held[at(last_ref[(p * 4 + t) * SLOTS + q])]
+            return held[last_ref[(p * 4 + t) * SLOTS + q]]
 
         half = HALF[p]
         shift = SHIFTS[t]
@@ -222,12 +235,105 @@
             for q in range(SLOTS):
                 pltpu.make_async_copy(*out_copy(p, q)).start()
 
+    def sum_all(t):
+        load(t, 0)
+        load(t, 1)
+        add_up(t, 0)
+        load(t, 2)
+        add_up(t, 1)
+        add_up(t, 2)
+
+    core0 = me["k"] == 0
+    at_root = (me["z"] == 0) & (me["y"] == 0) & (me["x"] == 0) & core0
+
+    def spread_inverse(event, p):
+        d, e, f = ORDERS[p]
+        start, size, width = BANDS[p]
+        part = square.at[pl.ds(start, size), pl.ds(0, width)]
+        on = (at_root, (me[e] == 0) & (me[f] == 0) & core0, (me[f] == 0) & core0, core0)
+
+        def sends(n):
+            axis = ORDERS[p][n // 2] if n < 6 else "k"
+            if n % 2 == 0:
+                senders = on[n // 2] if n == 6 else on[n // 2] & (me[axis] == 0)
+            else:
+                senders = on[n // 2 + 1] & (me[axis] == 1)
+            copies = [
+                pltpu.make_async_remote_copy(
+                    src_ref=part,
+                    dst_ref=part,
+                    send_sem=send_s.at[p, n, i],
+                    recv_sem=recv_s.at[p],
+                    device_id=device(moved(me, **{axis: step})),
+                    device_id_type=MESH,
+                )
+                for i, step in enumerate((1, 3) if n in (0, 2, 4) else (1,))
+            ]
+            return senders, copies
+
+        def receivers(n):
+            if n == 6:
+                return me["k"] == 1
+            axis = ORDERS[p][n // 2]
+            mine = on[n // 2 + 1]
+            if n % 2 == 0:
+                return mine & ((me[axis] == 1) | (me[axis] == 3))
+            return mine & (me[axis] == 2)
+
+        if event > 0:
+
+            @pl.when(receivers(event - 1))
+            def _():
+                pltpu.make_async_copy(part, part, recv_s.at[p]).wait()
+
+            senders, copies = sends(event - 1)
+
+            @pl.when(senders)
+            def _():
+                for copy in copies:
+                    copy.wait_send()
+
+        if event < 7:
+            senders, copies = sends(event)
+
+            @pl.when(senders)
+            def _():
+                for copy in copies:
+                    copy.start()
+
+    def factor_steps(low, high):
+        @pl.when(at_root)
+        def _():
+            if low == 0:
+                corner = front.at[pl.ds(0, P_SIZE), pl.ds(0, P_SIZE)]
+                copy = pltpu.make_async_copy(corner, work, corner_sem.at[0])
+                copy.start()
+                copy.wait()
+            factor_blocks(work, inverse, low, high)
+            if high == 4:
+                copies = [pltpu.make_async_copy(work, factor_out, corner_sem.at[0])]
+                for p in range(3):
+                    start, size, width = BANDS[p]
+                    copies.append(
+                        pltpu.make_async_copy(
+                            inverse.at[pl.ds(start, size), pl.ds(0, width)],
+                            square.at[pl.ds(start, size), pl.ds(0, width)],
+                            corner_sem.at[p + 1],
+                        )
+                    )
+                for copy in copies:
+                    copy.start()
+                for copy in copies:
+                    copy.wait()
+
     for p in range(3):
         pack(0, p)
-        got[p][4] = jnp.zeros((8, 2, ROWS[p], 128), jnp.float32)
+    for pool in pools:
+        pool[64] = jnp.zeros((max(ROWS), 128), jnp.float32)
     pl.semaphore_wait(barrier, len(partners))
     for p in range(3):
         start_a(0, p)
+    factor_steps(0, 2)
     for t in range(4):
         for p in range(3):
             start_b(t, p)
@@ -235,19 +341,20 @@
                 wait_send_a(t, p)
                 pack(t + 1, p)
                 start_a(t + 1, p)
-        if t > 0:
+        if t == 0:
+            factor_steps(2, 4)
+        else:
             for p in range(3):
-                load(t - 1, p)
-            for p in range(3):
-                add_up(t - 1, p)
+                spread_inverse(2 * t - 1, p)
+            sum_all(t - 1)
+        for p in range(3):
+            spread_inverse(2 * t, p)
+    sum_all(3)
     for p in range(3):
-        load(3, p)
-    for p in range(3):
-        add_up(3, p)
-    for p in range(3):
+        spread_inverse(7, p)
         wait_send_a(3, p)
         for t in range(4):
-            part = middle[p].at[t, pl.ds(0, 3)]
+            part = middle[p].at[t, pl.ds(0, 48)]
             pltpu.make_async_copy(part, part, send_b.at[t, p]).wait()
         whole = far[p]
         pltpu.make_async_copy(whole, whole, out_sem.at[p]).wait()
@@ -256,27 +363,32 @@
 def exchange(where, prev, last, child_tiles, front_matrix):
     f32 = jnp.float32
     scratch = [pltpu.VMEM((8, 4, 2, r, 128), f32) for r in ROWS]
-    scratch += [pltpu.VMEM((5, 8, 2, r, 128), f32) for r in ROWS]
+    scratch += [pltpu.VMEM((65, max(ROWS), 128), f32)] * 2
     for _ in range(6):
         scratch += [pltpu.VMEM((SLOTS, r, 128), f32) for r in ROWS]
     scratch += [pltpu.SemaphoreType.DMA((4, 3))] * 6
     scratch += [pltpu.SemaphoreType.DMA((3,))] * 3
+    scratch += [pltpu.SemaphoreType.DMA((3, 7, 2)), pltpu.SemaphoreType.DMA((3,))]
+    scratch += [pltpu.SemaphoreType.DMA((4,))]
+    scratch += [pltpu.VMEM((P_SIZE, P_SIZE), f32)] * 2
     anywhere = pl.BlockSpec(memory_space=pl.ANY)
     outs = [jax.ShapeDtypeStruct(front_matrix.shape, f32)]
-    outs += [jax.ShapeDtypeStruct((4, 4, 8, 2, r, 128), f32) for r in ROWS]
-    outs += [jax.ShapeDtypeStruct((4, 4, 8, 2, r, 128), f32) for r in ROWS]
-    return pl.pallas_call(
+    outs += [jax.ShapeDtypeStruct((4, 4, 16, r, 128), f32) for r in ROWS]
+    outs += [jax.ShapeDtypeStruct((4, 64, r, 128), f32) for r in ROWS]
+    outs += [jax.ShapeDtypeStruct((P_SIZE, P_SIZE), f32)] * 2
+    results = pl.pallas_call(
         exchange_kernel,
         out_shape=outs,
         in_specs=[pl.BlockSpec(memory_space=pltpu.SMEM)] * 3
         + [pl.BlockSpec(memory_space=pltpu.VMEM), anywhere],
-        out_specs=[anywhere] * 7,
+        out_specs=[anywhere] * 9,
         scratch_shapes=scratch,
         compiler_params=pltpu.CompilerParams(
-            collective_id=1, has_side_effects=True, vmem_limit_bytes=62 << 20
+            collective_id=1, has_side_effects=True, vmem_limit_bytes=(63 << 20) + (1 << 19)
         ),
         name="exchange",
-    )(where, prev, last, child_tiles, front_matrix)[0]
+    )(where, prev, last, child_tiles, front_matrix)
+    return results[0], results[7], results[8]
 
 
 def routing(owner_index, slot_index):
@@ -288,7 +400,8 @@
     hit = place[:, None] == lax.broadcasted_iota(jnp.int32, (count, 256), 1)
     where = jnp.sum(jnp.where(hit, lax.broadcasted_iota(jnp.int32, hit.shape, 0), 0), axis=0)
     slots = jnp.sum(jnp.where(hit, slot_index[:, None] + 1, 0), axis=0) - 1
-    table = lax.all_gather(slots.astype(jnp.float32), ("row", "col"))
+    own = jnp.concatenate([slots.reshape(2, 128), jnp.zeros((6, 128), jnp.int32)], 0)
+    table = share_table(own).reshape(128, 8, 128)[:, 0:2].reshape(128, 256).astype(jnp.float32)
     me = position()
     pick_source, pick_owner = [], []
     source = jnp.arange(128)
@@ -338,68 +451,328 @@
     return where, prev.reshape(-1), last.reshape(-1)
 
 
-def assemble(front_matrix, child_tiles, owner_index, slot_index):
+def line(me, axis):
+    return [moved(me, **{axis: step}) for step in (1, 3, 2)]
+
+
+def file(me):
+    near = [moved(me, z=step, k=core) for step, core in ((1, 0), (3, 0), (1, 1), (3, 1), (2, 0), (2, 1))]
+    return near + [moved(me, k=1)]
+
+
+def greet(barrier, partners):
+    for to in partners:
+        pl.semaphore_signal(barrier, inc=1, device_id=device(to), device_id_type=MESH)
+
+
+def table_kernel(own, table, send, recv):
+    me = position()
+    barrier = pltpu.get_barrier_semaphore()
+    partners = file(me) + line(me, "y") + line(me, "x")
+    greet(barrier, partners)
+    r = me["z"] * 2 + me["k"]
+    table[r, me["y"], me["x"]] = own[...]
+    pl.semaphore_wait(barrier, len(partners))
+
+    def run(stage, part, targets):
+        copies = [
+            pltpu.make_async_remote_copy(
+                src_ref=part,
+                dst_ref=part,
+                send_sem=send.at[stage, i],
+                recv_sem=recv.at[stage, i],
+                device_id=device(to),
+                device_id_type=MESH,
+            )
+            for i, to in enumerate(targets)
+        ]
+        for copy in copies:
+            copy.start()
+        for copy in copies:
+            copy.wait()
+
+    run(0, table.at[r, me["y"], me["x"]], file(me))
+    run(1, table.at[:, me["y"], me["x"]], line(me, "y"))
+    run(2, table.at[:, :, me["x"]], line(me, "x"))
+
+
+def share_table(own):
+    return pl.pallas_call(
+        table_kernel,
+        out_shape=jax.ShapeDtypeStruct((8, 4, 4, 8, 128), jnp.int32),
+        in_specs=[pl.BlockSpec(memory_space=pltpu.VMEM)],
+        out_specs=pl.BlockSpec(memory_space=pltpu.VMEM),
+        scratch_shapes=[pltpu.SemaphoreType.DMA((3, 7))] * 2,
+        compiler_params=pltpu.CompilerParams(collective_id=2, has_side_effects=True),
+        name="share_table",
+    )(own)
+
+
+def panel_kernel(assembled, rows, columns, send0, recv0, send1, recv1, send_x, recv_x, send_y, recv_y, send_z, recv_z):
+    me = position()
+    r = me["z"] * 2 + me["k"]
+    y, x = me["y"], me["x"]
+    c = y * 4 + x
+    depth = rows.shape[2]
+    half = depth // 2
+    barrier = pltpu.get_barrier_semaphore()
+    first = c == 0
+    to_row, to_col = lax.rem(c, 8), 2 * r + c // 8
+    from_row, from_col = c // 2, r + 8 * lax.rem(c, 2)
+    stays = (to_row == r) & (to_col == c)
+    partners = file(me) + line(me, "y") + line(me, "x")
+    greet(barrier, partners)
+
+    @pl.when(c != 0)
+    def _():
+        pl.semaphore_signal(barrier, inc=1, device_id=(r, 0), device_id_type=MESH)
+
+    @pl.when(jnp.logical_not(stays))
+    def _():
+        pl.semaphore_signal(barrier, inc=1, device_id=(from_row, from_col), device_id_type=MESH)
+
+    others = jnp.where(first, 15, 0) + jnp.where(stays, 0, 1)
+    pl.semaphore_wait(barrier, len(partners) + others)
+
+    @pl.when(first)
+    def _():
+        for j in (5, 10, 15, 1, 4, 3, 12, 6, 9, 7, 13, 11, 14, 2, 8):
+            pltpu.make_async_remote_copy(
+                src_ref=assembled.at[pl.ds(j * depth, depth), pl.ds(0, P_SIZE)],
+                dst_ref=rows.at[j // 4, j % 4],
+                send_sem=send0,
+                recv_sem=recv0,
+                device_id=(r, j),
+                device_id_type=MESH,
+            ).start()
+        pltpu.make_async_copy(
+            assembled.at[pl.ds(0, depth), pl.ds(0, P_SIZE)], rows.at[0, 0], recv0
+        ).start()
+
+    mine = rows.at[y, x]
+    pltpu.make_async_copy(mine, mine, recv0).wait()
+
+    low, high = pl.ds(0, half), pl.ds(half, depth - half)
+
+    def spread(part, targets, send, recv):
+        copies = [
+            pltpu.make_async_remote_copy(
+                src_ref=part,
+                dst_ref=part,
+                send_sem=send.at[i],
+                recv_sem=recv.at[i],
+                device_id=device(to),
+                device_id_type=MESH,
+            )
+            for i, to in enumerate(targets)
+        ]
+        for copy in copies:
+            copy.start()
+        return copies
+
+    def finish(copies):
+        for copy in copies:
+            copy.wait()
+
+    @pl.when(jnp.logical_not(stays))
+    def _():
+        pltpu.make_async_remote_copy(
+            src_ref=mine,
+            dst_ref=columns.at[to_row],
+            send_sem=send1,
+            recv_sem=recv1,
+            device_id=(to_row, to_col),
+            device_id_type=MESH,
+        ).start()
+
+    @pl.when(stays)
+    def _():
+        pltpu.make_async_copy(mine, columns.at[r], recv1).start()
+
+    a1 = spread(rows.at[y, x, low], line(me, "x"), send_x.at[0], recv_x.at[0])
+    b1 = spread(rows.at[y, x, high], line(me, "y"), send_y.at[0], recv_y.at[0])
+    held = columns.at[r]
+    pltpu.make_async_copy(held, held, recv1).wait()
+    z1 = spread(held, file(me), send_z, recv_z)
+    finish(a1)
+    a2 = spread(rows.at[y, :, low], line(me, "y"), send_y.at[1], recv_y.at[1])
+    finish(b1)
+    b2 = spread(rows.at[:, x, high], line(me, "x"), send_x.at[1], recv_x.at[1])
+    finish(z1)
+    finish(a2)
+    finish(b2)
+
+    @pl.when(jnp.logical_not(stays))
+    def _():
+        pltpu.make_async_copy(mine, mine, send1).wait()
+
+    @pl.when(first)
+    def _():
+        whole = assembled.at[pl.ds(depth, 15 * depth), pl.ds(0, P_SIZE)]
+        pltpu.make_async_copy(whole, whole, send0).wait()
+
+
+def share_panel(assembled):
+    depth = assembled.shape[0] // 16
+    anywhere = pl.BlockSpec(memory_space=pl.ANY)
+    dma = pltpu.SemaphoreType.DMA
+    return pl.pallas_call(
+        panel_kernel,
+        out_shape=[
+            jax.ShapeDtypeStruct((4, 4, depth, P_SIZE), jnp.float32),
+            jax.ShapeDtypeStruct((8, depth, P_SIZE), jnp.float32),
+        ],
+        in_specs=[anywhere],
+        out_specs=[anywhere] * 2,
+        scratch_shapes=[dma, dma, dma, dma, dma((2, 3)), dma((2, 3)), dma((2, 3)), dma((2, 3)), dma((7,)), dma((7,))],
+        compiler_params=pltpu.CompilerParams(collective_id=3, has_side_effects=True),
+        name="share_panel",
+    )(assembled)
+
+
+def factor_blocks(work, inverse, first, last):
+    n = P_SIZE
+    f32 = jnp.float32
+    highest = lax.Precision.HIGHEST
+
+    def times(a, b, dims):
+        return lax.dot_general(a, b, (dims, ((), ())), precision=highest, preferred_element_type=f32)
+
+    if first == 0:
+        block = work[...]
+        work[...] = 0.5 * (block + block.T)
+        inverse[...] = jnp.zeros((n, n), f32)
+    row128 = lax.broadcasted_iota(jnp.int32, (128, 128), 0)
+    col128 = lax.broadcasted_iota(jnp.int32, (128, 128), 1)
+    row8 = lax.broadcasted_iota(jnp.int32, (8, 1), 0)
+
+    def step(b, carry):
+        here = pl.ds(pl.multiple_of(b * 128, 128), 128)
+        corner = work[here, here]
+        eye = (row128 == col128).astype(f32)
+        up = [corner[8 * g : 8 * g + 8] for g in range(16)]
+        low = [eye[8 * g : 8 * g + 8] for g in range(16)]
+        for j in range(128):
+            g, s = j // 8, j % 8
+            pivot = up[g][s : s + 1, j : j + 1]
+            scale = 1.0 / pivot
+            row = up[g][s : s + 1] * scale
+            other = low[g][s : s + 1] * scale
+            for i in range(g, 16):
+                column = up[i][:, j : j + 1]
+                if i == g:
+                    column = jnp.where(row8 > s, column, 0.0)
+                up[i] = up[i] - column * row
+                low[i] = low[i] - column * other
+        upper = jnp.concatenate(up, 0)
+        lower = jnp.concatenate(low, 0)
+        pivots = jnp.sum(jnp.where(row128 == col128, upper, 0.0), axis=1, keepdims=True)
+        scale = lax.rsqrt(pivots)
+        corner_factor = jnp.where(row128 <= col128, upper * scale, 0.0).T
+        corner_inverse = jnp.where(row128 >= col128, lower * scale, 0.0)
+        below = times(work[:, here], corner_inverse, ((1,), (1,)))
+        row = lax.broadcasted_iota(jnp.int32, (n, 128), 0)
+        below = jnp.where(row >= b * 128 + 128, below, 0.0)
+        work[...] = work[...] - times(below, below, ((1,), (1,)))
+        done = lax.broadcasted_iota(jnp.int32, (128, n), 1) < b * 128
+        left = times(jnp.where(done, work[here, :], 0.0), inverse[...], ((1,), (0,)))
+        inverse[here, :] = -times(corner_inverse, left, ((1,), (0,)))
+        inverse[here, here] = corner_inverse
+        work[:, here] = below
+        work[here, here] = corner_factor
+        return carry
+
+    lax.fori_loop(first, last, step, 0)
+
+
+def split(value):
+    high = value.astype(jnp.bfloat16)
+    low = (value - high.astype(jnp.float32)).astype(jnp.bfloat16)
+    return high, low
+
+
+def product(a, b):
+    def times(x, y):
+        return lax.dot_general(x, y, (((1,), (1,)), ((), ())), preferred_element_type=jnp.float32)
+
+    return times(a[0], b[0]) + (times(a[0], b[1]) + times(a[1], b[0]))
+
+
+def update_kernel(place, rows_raw, columns_raw, inverse, factor, assembled, out, inv_hi, inv_lo, col_hi, col_lo):
+    step = pl.program_id(0)
+    tile, width = out.shape
+
+    @pl.when(step == 0)
+    def _():
+        row = lax.broadcasted_iota(jnp.int32, inverse.shape, 0)
+        col = lax.broadcasted_iota(jnp.int32, inverse.shape, 1)
+        high, low = split(jnp.where(row >= col, inverse[...], 0.0))
+        inv_hi[...] = high
+        inv_lo[...] = low
+        high, low = split(product(split(columns_raw[...]), (high, low)))
+        col_hi[...] = high
+        col_lo[...] = low
+
+    row_start = place[0] + step * tile
+    col_start = place[1]
+    panel = product(split(rows_raw[...]), (inv_hi[...], inv_lo[...]))
+    change = product(split(panel), (col_hi[...], col_lo[...]))
+    row = row_start + lax.broadcasted_iota(jnp.int32, (tile, width), 0)
+    col = col_start + lax.broadcasted_iota(jnp.int32, (tile, width), 1)
+    out[...] = assembled[...] - jnp.where((row >= col) & (col >= P_SIZE), change, 0.0)
+
+    @pl.when(col_start == 0)
+    def _():
+        out[:, 0:P_SIZE] = panel
+
+    @pl.when((col_start == 0) & (row_start < P_SIZE))
+    def _():
+        out[:, 0:P_SIZE] = factor[...]
+
+
+def update(place, rows_raw, columns_raw, inverse, factor, assembled):
+    rows, width = assembled.shape
+    tile = 256
+    whole = lambda shape: pl.BlockSpec(shape, lambda i: (0, 0))
+    bf16 = jnp.bfloat16
+    return pl.pallas_call(
+        update_kernel,
+        grid=(rows // tile,),
+        out_shape=jax.ShapeDtypeStruct((rows, width), jnp.float32),
+        in_specs=[
+            pl.BlockSpec(memory_space=pltpu.SMEM),
+            pl.BlockSpec((tile, P_SIZE), lambda i: (i, 0)),
+            whole((width, P_SIZE)),
+            whole((P_SIZE, P_SIZE)),
+            pl.BlockSpec((tile, P_SIZE), lambda i: (jnp.minimum(i, P_SIZE // tile - 1), 0)),
+            pl.BlockSpec((tile, width), lambda i: (i, 0)),
+        ],
+        out_specs=pl.BlockSpec((tile, width), lambda i: (i, 0)),
+        scratch_shapes=[
+            pltpu.VMEM((P_SIZE, P_SIZE), bf16),
+            pltpu.VMEM((P_SIZE, P_SIZE), bf16),
+            pltpu.VMEM((width, P_SIZE), bf16),
+            pltpu.VMEM((width, P_SIZE), bf16),
+        ],
+        compiler_params=pltpu.CompilerParams(vmem_limit_bytes=48 << 20),
+        name="update",
+    )(place, rows_raw, columns_raw, inverse, factor, assembled)
+
+
+def local(front_matrix, child_tiles, owner_index, slot_index):
     where, prev, last = routing(owner_index, slot_index)
-    return exchange(where, prev, last, child_tiles, front_matrix)
-
-
-def spread(block, axis, source):
-    block = jnp.where(lax.axis_index(axis) == source, block, jnp.zeros_like(block))
-    return lax.psum(block, axis)
-
-
-def factor_block(block):
-    factor = jnp.linalg.cholesky(0.5 * (block + block.T))
-    identity = jnp.eye(block.shape[0], dtype=jnp.float32)
-    inverse = jax.scipy.linalg.solve_triangular(factor, identity, lower=True)
-    return (jnp.tril(factor), inverse)
-
-
-def solve_panel(columns, factor, inverse, row_start):
-    solved = lax.dot_general(
-        columns,
+    assembled, inverse, factor = exchange(where, prev, last, child_tiles, front_matrix)
+    rows, columns = share_panel(assembled)
+    rows_loc, cols_loc = front_matrix.shape
+    place = jnp.stack([lax.axis_index("row") * rows_loc, lax.axis_index("col") * cols_loc])
+    return update(
+        place.astype(jnp.int32),
+        rows.reshape(rows_loc, P_SIZE),
+        columns.reshape(cols_loc, P_SIZE),
         inverse,
-        (((1,), (1,)), ((), ())),
-        precision=lax.Precision.HIGHEST,
-        preferred_element_type=jnp.float32,
+        factor,
+        assembled,
     )
-    panel_size = factor.shape[0]
-    padded = jnp.concatenate(
-        [factor, jnp.zeros((columns.shape[0] - panel_size, panel_size), jnp.float32)], 0
-    )
-    global_row = row_start + lax.broadcasted_iota(jnp.int32, solved.shape, 0)
-    return jnp.where(global_row < panel_size, padded, solved)
-
-
-def local(front_matrix, child_tiles, owner_index, slot_index):
-    rows_loc, cols_loc = front_matrix.shape
-    assembled = assemble(front_matrix, child_tiles, owner_index, slot_index)
-    my_row = lax.axis_index("row")
-    my_col = lax.axis_index("col")
-    row_start = my_row * rows_loc
-    diagonal = spread(assembled[:P_SIZE, :P_SIZE], "row", 0)
-    diagonal = jnp.where(my_col == 0, diagonal, jnp.eye(P_SIZE, dtype=jnp.float32))
-    factor, inverse = factor_block(diagonal)
-    own_panel = solve_panel(assembled[:, :P_SIZE], factor, inverse, row_start)
-    panel_rows = spread(own_panel, "col", 0)
-    offset = my_col * cols_loc % rows_loc
-    root_row = my_col * cols_loc // rows_loc
-    column_piece = lax.dynamic_slice_in_dim(panel_rows, offset, cols_loc, 0)
-    column_rows = spread(column_piece, "row", root_row)
-    update = lax.dot_general(
-        panel_rows,
-        column_rows,
-        (((1,), (1,)), ((), ())),
-        precision=lax.Precision.HIGHEST,
-        preferred_element_type=jnp.float32,
-    )
-    global_row = row_start + lax.broadcasted_iota(jnp.int32, (rows_loc, cols_loc), 0)
-    global_col = my_col * cols_loc + lax.broadcasted_iota(jnp.int32, (rows_loc, cols_loc), 1)
-    lowered = jnp.where(global_row >= global_col, assembled - update, assembled)
-    panel_wide = jnp.concatenate(
-        [panel_rows, jnp.zeros((rows_loc, cols_loc - P_SIZE), jnp.float32)], 1
-    )
-    return jnp.where(global_col < P_SIZE, panel_wide, lowered)
 
 
 def solution(mesh):

time: 813 us -> 446 us (0.55)
  waiting for transfers between devices: 219 us -> 0 us
  other arithmetic: 134 us -> 5.65 us
  Pallas kernels: 321 us -> 433 us
  blocking collectives: 57.7 us -> 0 us
  matrix products: 29.6 us -> 0.77 us
  local copies, waits for them, and re-layouts: 29.2 us -> 6.32 us
  between operations: 16.4 us -> 0.16 us
    psum x3 -> x0, waiting for transfers between devices: 219 us -> none  [spread(): return lax.psum(block, axis)]
    another operation x17 -> x1, other arithmetic: 120 us -> 0.07 us  [local(): jnp.stack([lax.axis_index('row') * rows_loc, lax.axis_index('col') * cols...]
    pallas_call x0 -> x3, Pallas kernels: none -> 114 us  [the longest x1 76.3 us: share_panel(): pl.pallas_call(panel_kernel, out_shape=[jax.ShapeDtypeStruct((4, 4, depth...]
    all_gather x1 -> x0, blocking collectives: 57.7 us -> none  [routing(): table = lax.all_gather(slots.astype(jnp.float32), ('row', 'col'))]
    dot_general x2 -> x0, matrix products: 20.3 us -> none  [the longest x1 12.1 us: local(): lax.dot_general(panel_rows, column_rows, (((1,), (1,)), ((), ())), precis...]
    another operation x34 -> x0, local copies, waits for them, and re-layouts: 14.5 us -> none
    another operation x13 -> x0, matrix products: 8.59 us -> none  [the longest x7 5.43 us: factor_block(): inverse = jax.scipy.linalg.solve_triangular(factor, identity, lower=True)]
  transfers between devices with their start and end apart: 3 -> 0, of which waited for: 3 -> 0; matrix products, arithmetic and copies ran while one was open for 0% -> 0% of each run, Pallas kernels for 0% -> 0%
where the time goes in v2:
time: 446 us
  Pallas kernels  433 us (97%)
  local copies, waits for them, and re-layouts  6.32 us (1%)
  other arithmetic  5.65 us (1%)
    pallas_call x1, Pallas kernels, exchange(): pl.pallas_call(exchange_kernel, out_shape=outs, in_specs=[pl.BlockSpec(me...  319 us
    pallas_call x1, Pallas kernels, share_panel(): pl.pallas_call(panel_kernel, out_shape=[jax.ShapeDtypeStruct((4, 4, depth...  76.3 us
    pallas_call x1, Pallas kernels, share_table(): pl.pallas_call(table_kernel, out_shape=jax.ShapeDtypeStruct((8, 4, 4, 8,...  23.5 us
    pallas_call x1, Pallas kernels, update(): pl.pallas_call(update_kernel, grid=(rows // tile,), out_shape=jax.ShapeDt...  13.8 us

profile of v2, /device:TPU:0, one launch (start us, length us, event | category | flops | bytes accessed | tf_op | source)
XLA Modules:
  0.0 445.6 jit_solution(7931742821700025318)
XLA Ops:
  0.1 0.9 convert_reduce_fusion
  1.1 0.7 multiply_add_fusion
  1.7 0.7 select_reduce_fusion.2
  2.5 0.6 concatenate.8.own
  3.1 1.3 gather_fusion
  4.4 0.1 fusion.16
  4.5 23.5 %share_table.1 = s32[8,4,4,8,128]{4,3,2,1,0:T(8,128)} custom-call(s32[8,128]{1,0:T(8,128)} %concatenate.8.own), custom_call_target="tpu_custom_call" | custom-call | tf_op jit(solution)/shard_map/share_table/pallas_call | solution.py:500
  28.0 1.1 slice_convert_fusion
  29.1 0.2 fusion.1
  29.3 0.2 fusion.10
  29.5 0.2 fusion.12
  29.7 0.2 fusion.14
  29.9 0.1 copy.34
  30.1 0.1 convert_element_type.38
  30.4 0.5 select_reduce_fusion
  31.0 0.6 compare_select_fusion.prev_ref
  31.6 0.3 select_reduce_fusion.1
  31.9 0.6 compare_select_fusion.1.last_ref
  32.5 319.1 %exchange.1 = (f32[1536,768]{1,0:T(8,128)}, f32[4,4,16,88,128]{4,3,2,1,0:T(8,128)}, f32[4,4,16,88,128]{4,3,2,1,0:T(8,128)}, f32[4,4,16,80,128]{4,3,2,1,0:T(8,128...) custom-call(s32[256]{0:T(256)} %get-tuple-element.16.where_ref, ...), custom_call_target="tpu_custom_call" | custom-call | tf_op jit(solution)/shard_map/exchange/pallas_call | solution.py:379
  351.7 76.3 %share_panel.1 = (f32[4,4,96,512]{3,2,1,0:T(8,128)}, f32[8,96,512]{2,1,0:T(8,128)}) custom-call(f32[1536,768]{1,0:T(8,128)} %get-tuple-element.10.assembled), custom_call_target="tpu_custom_call" | custom-call | tf_op jit(solution)/shard_map/share_panel/pallas_call | solution.py:619
  428.0 1.4 copy-done
  429.4 1.2 copy-done.1
  430.6 1.2 copy-done.2
  431.8 13.8 %update.1 = f32[1536,768]{1,0:T(8,128)} custom-call(s32[2]{0:T(128)S(1)} %pad_add_fusion.place, f32[1536,512]{1,0:T(8,128)} %bitcast.21, f32[768,512]{1,0:T(8,128)S(1)} %bitcast.20, f32[512,512]{1,0:T(8,128)S(1)} %copy-done.1, f32[512,512]{1,0:T(8,128)S(1)} %copy-done.2, f32[1536,768]{1,0:T(8,128)} %get-tuple-element.10.assembled), custom_call_target="tpu_custom_call" | custom-call | tf_op jit(solution)/shard_map/update/pallas_call | solution.py:738
  (28 shorter events, 0.5 us)
Async XLA Ops:
  427.9 1.4 copy-start
  429.4 1.2 copy-start.1
  430.6 1.2 copy-start.2

commit v3 on v2

--- a/solution.py
+++ b/solution.py
@@ -37,8 +37,7 @@
 
 def exchange_kernel(
     where_ref,
-    prev_ref,
-    last_ref,
+    own_ref,
     child,
     front,
     out,
@@ -50,6 +49,7 @@
     mid2,
     square,
     factor_out,
+    tables,
     *scratch,
 ):
     arrived = (arr0, arr1, arr2)
@@ -59,7 +59,8 @@
     far, right, left = scratch[5:8], scratch[8:11], scratch[11:14]
     in_far, in_left, in_right = scratch[14:17], scratch[17:20], scratch[20:23]
     send_a, recv_a, send_b, recv_b, send_c, recv_c, load_sem, front_sem, out_sem = scratch[23:32]
-    send_s, recv_s, corner_sem, work, inverse = scratch[32:]
+    send_s, recv_s, corner_sem, work, inverse, *more = scratch[32:]
+    send_t, recv_t, near_t, gathered, tab_vector, tab = more
     me = position()
 
     barrier = pltpu.get_barrier_semaphore()
@@ -172,13 +173,13 @@
         ).wait()
 
         def chain(k, carry):
-            held[k] = held[k] + held[prev_ref[(p * 4 + t) * 64 + k]]
+            held[k] = held[k] + held[tab[t, 2 * p, k]]
             return carry
 
         lax.fori_loop(0, 64, chain, 0)
 
         def total(q):
-            return held[last_ref[(p * 4 + t) * SLOTS + q]]
+            return held[tab[t, 2 * p + 1, q]]
 
         half = HALF[p]
         shift = SHIFTS[t]
@@ -326,13 +327,125 @@
                 for copy in copies:
                     copy.wait()
 
+    row_here = me["z"] * 2 + me["k"]
+
+    def table_copies(stage):
+        if stage == 0:
+            part = tables.at[row_here, me["y"], me["x"]]
+            source = own_ref
+            targets = [moved(me, z=step, k=core) for step in (1, 3, 2) for core in (0, 1)]
+            targets.append(moved(me, k=1))
+        elif stage == 1:
+            source = part = tables.at[pl.ds(0, 8), me["y"], me["x"]]
+            targets = [moved(me, y=step) for step in (1, 3, 2)]
+        else:
+            source = part = tables.at[pl.ds(0, 8), pl.ds(0, 4), me["x"]]
+            targets = [moved(me, x=step) for step in (1, 3, 2)]
+        return [
+            pltpu.make_async_remote_copy(
+                src_ref=source,
+                dst_ref=part,
+                send_sem=send_t.at[stage, i],
+                recv_sem=recv_t.at[stage],
+                device_id=device(to),
+                device_id_type=MESH,
+            )
+            for i, to in enumerate(targets)
+        ]
+
+    def share_table(stage):
+        if stage == 0:
+            pltpu.make_async_copy(
+                own_ref, tables.at[row_here, me["y"], me["x"]], recv_t.at[0]
+            ).start()
+        elif stage == 1:
+            part = tables.at[pl.ds(0, 8), me["y"], me["x"]]
+            pltpu.make_async_copy(part, part, recv_t.at[0]).wait()
+        elif stage == 2:
+            part = tables.at[pl.ds(0, 8), pl.ds(0, 3), me["x"]]
+            pltpu.make_async_copy(part, part, recv_t.at[1]).wait()
+        else:
+            part = tables.at[pl.ds(0, 8), pl.ds(0, 4), pl.ds(0, 3)]
+            pltpu.make_async_copy(part, part, recv_t.at[2]).wait()
+        if stage < 3:
+            for copy in table_copies(stage):
+                copy.start()
+
+    def make_tables():
+        for p in range(3):
+            d, e, f = ORDERS[p]
+            copies = []
+            for step in range(4):
+                if p == 0:
+                    pieces = [(tables.at[pl.ds(0, 8), me["y"], step], step * 8, 8)]
+                elif p == 1:
+                    pieces = [
+                        (tables.at[me["z"] * 2 + k, step, pl.ds(0, 4)], step * 8 + k * 4, 4)
+                        for k in range(2)
+                    ]
+                else:
+                    pieces = [
+                        (tables.at[step * 2 + k, pl.ds(0, 4), me["x"]], step * 8 + k * 4, 4)
+                        for k in range(2)
+                    ]
+                for source, start, size in pieces:
+                    copies.append(
+                        pltpu.make_async_copy(
+                            source, gathered.at[pl.ds(start, size)], near_t.at[len(copies)]
+                        )
+                    )
+            for copy in copies:
+                copy.start()
+            for copy in copies:
+                copy.wait()
+            entry = lax.broadcasted_iota(jnp.int32, (64, 128), 0)
+            lane = lax.broadcasted_iota(jnp.int32, (64, 128), 1)
+            source = lax.rem(entry, 32)
+            if p > 0:
+                source = source // 8 * 8 + lax.rem(source, 4) * 2 + lax.rem(source // 4, 2)
+            order = source * 2 + entry // 32
+            for t in range(4):
+                at = dict(me)
+                at[f] = lax.rem(me[f] + SHIFTS[t], 4)
+                place = (((at["z"] * 2 + at["k"]) * 4 + at["y"]) * 4 + at["x"]) * 2
+                sub = lax.broadcasted_iota(jnp.int32, (32, 8, 128), 1)
+                picked = jnp.sum(jnp.where(sub == place // 128, gathered[...], 0), axis=1)
+                column = lax.rem(place, 128)
+                lane32 = lax.broadcasted_iota(jnp.int32, (32, 128), 1)
+                slots = jnp.concatenate(
+                    [
+                        jnp.broadcast_to(
+                            jnp.sum(
+                                jnp.where(lane32 == column + c, picked, 0), axis=1, keepdims=True
+                            ),
+                            (32, 128),
+                        )
+                        for c in range(2)
+                    ],
+                    0,
+                )
+                in_row = jnp.sum(jnp.where(order == lane, slots, 0), axis=0, keepdims=True)
+                match = (slots == in_row) & (slots >= 0) & (order < lane)
+                prev = jnp.max(jnp.where(match, order, -1), axis=0, keepdims=True)
+                last = jnp.max(jnp.where(slots == lane, order, -1), axis=0, keepdims=True)
+                tab_vector[t, 2 * p : 2 * p + 1, :] = jnp.where(prev < 0, 64, prev)
+                tab_vector[t, 2 * p + 1 : 2 * p + 2, :] = jnp.where(last < 0, 64, last)
+        copy = pltpu.make_async_copy(tab_vector, tab, near_t.at[0])
+        copy.start()
+        copy.wait()
+        for stage in range(3):
+            for copy in table_copies(stage):
+                copy.wait_send()
+
     for p in range(3):
         pack(0, p)
     for pool in pools:
         pool[64] = jnp.zeros((max(ROWS), 128), jnp.float32)
     pl.semaphore_wait(barrier, len(partners))
+    share_table(0)
     for p in range(3):
         start_a(0, p)
+    share_table(1)
     factor_steps(0, 2)
     for t in range(4):
         for p in range(3):
@@ -342,10 +455,14 @@
                 pack(t + 1, p)
                 start_a(t + 1, p)
         if t == 0:
+            share_table(2)
             factor_steps(2, 4)
         else:
             for p in range(3):
                 spread_inverse(2 * t - 1, p)
+            if t == 1:
+                share_table(3)
+                make_tables()
             sum_all(t - 1)
         for p in range(3):
             spread_inverse(2 * t, p)
@@ -360,7 +477,7 @@
         pltpu.make_async_copy(whole, whole, out_sem.at[p]).wait()
 
 
-def exchange(where, prev, last, child_tiles, front_matrix):
+def exchange(where, own, child_tiles, front_matrix):
     f32 = jnp.float32
     scratch = [pltpu.VMEM((8, 4, 2, r, 128), f32) for r in ROWS]
     scratch += [pltpu.VMEM((65, max(ROWS), 128), f32)] * 2
@@ -371,23 +488,28 @@
     scratch += [pltpu.SemaphoreType.DMA((3, 7, 2)), pltpu.SemaphoreType.DMA((3,))]
     scratch += [pltpu.SemaphoreType.DMA((4,))]
     scratch += [pltpu.VMEM((P_SIZE, P_SIZE), f32)] * 2
+    scratch += [pltpu.SemaphoreType.DMA((3, 7)), pltpu.SemaphoreType.DMA((3,))]
+    scratch += [pltpu.SemaphoreType.DMA((8,)), pltpu.VMEM((32, 8, 128), jnp.int32)]
+    scratch += [pltpu.VMEM((4, 8, 128), jnp.int32), pltpu.SMEM((4, 8, 128), jnp.int32)]
     anywhere = pl.BlockSpec(memory_space=pl.ANY)
     outs = [jax.ShapeDtypeStruct(front_matrix.shape, f32)]
     outs += [jax.ShapeDtypeStruct((4, 4, 16, r, 128), f32) for r in ROWS]
     outs += [jax.ShapeDtypeStruct((4, 64, r, 128), f32) for r in ROWS]
     outs += [jax.ShapeDtypeStruct((P_SIZE, P_SIZE), f32)] * 2
+    outs += [jax.ShapeDtypeStruct((8, 4, 4, 8, 128), jnp.int32)]
     results = pl.pallas_call(
         exchange_kernel,
         out_shape=outs,
-        in_specs=[pl.BlockSpec(memory_space=pltpu.SMEM)] * 3
-        + [pl.BlockSpec(memory_space=pltpu.VMEM), anywhere],
-        out_specs=[anywhere] * 9,
+        in_specs=[pl.BlockSpec(memory_space=pltpu.SMEM)]
+        + [pl.BlockSpec(memory_space=pltpu.VMEM)] * 2
+        + [anywhere],
+        out_specs=[anywhere] * 10,
         scratch_shapes=scratch,
         compiler_params=pltpu.CompilerParams(
             collective_id=1, has_side_effects=True, vmem_limit_bytes=(63 << 20) + (1 << 19)
         ),
         name="exchange",
-    )(where, prev, last, child_tiles, front_matrix)
+    )(where, own, child_tiles, front_matrix)
     return results[0], results[7], results[8]
 
 
@@ -401,54 +523,7 @@
     where = jnp.sum(jnp.where(hit, lax.broadcasted_iota(jnp.int32, hit.shape, 0), 0), axis=0)
     slots = jnp.sum(jnp.where(hit, slot_index[:, None] + 1, 0), axis=0) - 1
     own = jnp.concatenate([slots.reshape(2, 128), jnp.zeros((6, 128), jnp.int32)], 0)
-    table = share_table(own).reshape(128, 8, 128)[:, 0:2].reshape(128, 256).astype(jnp.float32)
-    me = position()
-    pick_source, pick_owner = [], []
-    source = jnp.arange(128)
-    source = {"z": source // 32, "k": source // 16 % 2, "y": source // 4 % 4, "x": source % 4}
-    place = jnp.arange(256)
-    target = {"z": place // 64, "k": place // 32 % 2, "y": place // 8 % 4, "x": place // 2 % 4}
-    for p in range(3):
-        d, e, f = ORDERS[p]
-        r = jnp.arange(32)
-        pick_source.append(
-            (source[e][None] == (r // 8)[:, None])
-            & (source[d][None] == (r // 2 % 4)[:, None])
-            & (source["k"][None] == (r % 2)[:, None])
-            & (source[f] == me[f])[None]
-        )
-        n = jnp.arange(8)
-        shift = jnp.array(SHIFTS)[n // 2]
-        pick_owner.append(
-            (target[d] == me[d])[:, None]
-            & (target["k"] == me["k"])[:, None]
-            & (target[e] == me[e])[:, None]
-            & (target[f][:, None] == ((me[f] + shift) % 4)[None])
-            & ((place % 2)[:, None] == (n % 2)[None])
-        )
-    rows = jnp.dot(
-        jnp.concatenate(pick_source, 0).astype(jnp.float32),
-        table,
-        precision=lax.Precision.HIGHEST,
-    )
-    entries = jnp.stack(
-        [
-            jnp.dot(rows[p * 32 : p * 32 + 32], pick_owner[p].astype(jnp.float32))
-            for p in range(3)
-        ]
-    )
-    entries = entries.reshape(3, 32, 4, 2).transpose(0, 2, 1, 3).reshape(12, 64)
-    entries = jnp.round(entries).astype(jnp.int32)
-    k = lax.broadcasted_iota(jnp.int32, (12, 64, 64), 1)
-    j = lax.broadcasted_iota(jnp.int32, (12, 64, 64), 2)
-    match = (entries[:, :, None] == entries[:, None, :]) & (entries[:, :, None] >= 0) & (j < k)
-    prev = jnp.max(jnp.where(match, j, -1), axis=2)
-    prev = jnp.where(prev < 0, 64, prev)
-    q = lax.broadcasted_iota(jnp.int32, (12, SLOTS, 64), 1)
-    j = lax.broadcasted_iota(jnp.int32, (12, SLOTS, 64), 2)
-    last = jnp.max(jnp.where(entries[:, None, :] == q, j, -1), axis=2)
-    last = jnp.where(last < 0, 64, last)
-    return where, prev.reshape(-1), last.reshape(-1)
+    return where, own
 
 
 def line(me, axis):
@@ -465,106 +540,115 @@
         pl.semaphore_signal(barrier, inc=1, device_id=device(to), device_id_type=MESH)
 
 
-def table_kernel(own, table, send, recv):
-    me = position()
-    barrier = pltpu.get_barrier_semaphore()
-    partners = file(me) + line(me, "y") + line(me, "x")
-    greet(barrier, partners)
-    r = me["z"] * 2 + me["k"]
-    table[r, me["y"], me["x"]] = own[...]
-    pl.semaphore_wait(barrier, len(partners))
-
-    def run(stage, part, targets):
-        copies = [
-            pltpu.make_async_remote_copy(
-                src_ref=part,
-                dst_ref=part,
-                send_sem=send.at[stage, i],
-                recv_sem=recv.at[stage, i],
-                device_id=device(to),
-                device_id_type=MESH,
-            )
-            for i, to in enumerate(targets)
-        ]
-        for copy in copies:
-            copy.start()
-        for copy in copies:
-            copy.wait()
-
-    run(0, table.at[r, me["y"], me["x"]], file(me))
-    run(1, table.at[:, me["y"], me["x"]], line(me, "y"))
-    run(2, table.at[:, :, me["x"]], line(me, "x"))
-
-
-def share_table(own):
-    return pl.pallas_call(
-        table_kernel,
-        out_shape=jax.ShapeDtypeStruct((8, 4, 4, 8, 128), jnp.int32),
-        in_specs=[pl.BlockSpec(memory_space=pltpu.VMEM)],
-        out_specs=pl.BlockSpec(memory_space=pltpu.VMEM),
-        scratch_shapes=[pltpu.SemaphoreType.DMA((3, 7))] * 2,
-        compiler_params=pltpu.CompilerParams(collective_id=2, has_side_effects=True),
-        name="share_table",
-    )(own)
-
-
-def panel_kernel(assembled, rows, columns, send0, recv0, send1, recv1, send_x, recv_x, send_y, recv_y, send_z, recv_z):
+def panel_kernel(
+    assembled, rows, columns, low_stage, high_stage, send0, recv0, send1, recv1, send2, recv2, send_x, recv_x, send_y, recv_y, send_z, recv_z
+):
     me = position()
     r = me["z"] * 2 + me["k"]
     y, x = me["y"], me["x"]
     c = y * 4 + x
     depth = rows.shape[2]
     half = depth // 2
+    low, high = pl.ds(0, half), pl.ds(half, depth - half)
+    wide = pl.ds(0, P_SIZE)
     barrier = pltpu.get_barrier_semaphore()
-    first = c == 0
     to_row, to_col = lax.rem(c, 8), 2 * r + c // 8
     from_row, from_col = c // 2, r + 8 * lax.rem(c, 2)
     stays = (to_row == r) & (to_col == c)
     partners = file(me) + line(me, "y") + line(me, "x")
     greet(barrier, partners)
 
-    @pl.when(c != 0)
-    def _():
-        pl.semaphore_signal(barrier, inc=1, device_id=(r, 0), device_id_type=MESH)
-
     @pl.when(jnp.logical_not(stays))
     def _():
         pl.semaphore_signal(barrier, inc=1, device_id=(from_row, from_col), device_id_type=MESH)
 
-    others = jnp.where(first, 15, 0) + jnp.where(stays, 0, 1)
-    pl.semaphore_wait(barrier, len(partners) + others)
-
-    @pl.when(first)
-    def _():
-        for j in (5, 10, 15, 1, 4, 3, 12, 6, 9, 7, 13, 11, 14, 2, 8):
-            pltpu.make_async_remote_copy(
-                src_ref=assembled.at[pl.ds(j * depth, depth), pl.ds(0, P_SIZE)],
-                dst_ref=rows.at[j // 4, j % 4],
-                send_sem=send0,
-                recv_sem=recv0,
-                device_id=(r, j),
-                device_id_type=MESH,
-            ).start()
-        pltpu.make_async_copy(
-            assembled.at[pl.ds(0, depth), pl.ds(0, P_SIZE)], rows.at[0, 0], recv0
-        ).start()
-
-    mine = rows.at[y, x]
-    pltpu.make_async_copy(mine, mine, recv0).wait()
-
-    low, high = pl.ds(0, half), pl.ds(half, depth - half)
+    pl.semaphore_wait(barrier, len(partners) + jnp.where(stays, 0, 1))
+
+    def remote(source, target, send, recv, to):
+        return pltpu.make_async_remote_copy(
+            src_ref=source,
+            dst_ref=target,
+            send_sem=send,
+            recv_sem=recv,
+            device_id=to,
+            device_id_type=MESH,
+        )
+
+    steps = (1, 3, 2)
+
+    def root_copies():
+        copies = []
+        for i, step in enumerate(steps):
+            copies.append(
+                remote(
+                    assembled.at[:, step, low, wide],
+                    low_stage,
+                    send0.at[0, i],
+                    recv0.at[0],
+                    device(moved(me, x=step)),
+                )
+            )
+            copies.append(
+                remote(
+                    assembled.at[step, :, high, wide],
+                    high_stage,
+                    send0.at[1, i],
+                    recv0.at[1],
+                    device(moved(me, y=step)),
+                )
+            )
+        return copies
+
+    def low_copies():
+        return [
+            remote(
+                low_stage.at[step],
+                rows.at[step, x, low],
+                send1.at[0, i],
+                recv1.at[0],
+                device(moved(me, y=step)),
+            )
+            for i, step in enumerate(steps)
+        ]
+
+    def high_copies():
+        return [
+            remote(
+                high_stage.at[step],
+                rows.at[y, step, high],
+                send1.at[1, i],
+                recv1.at[1],
+                device(moved(me, x=step)),
+            )
+            for i, step in enumerate(steps)
+        ]
+
+    at_top, at_side = y == 0, x == 0
+
+    @pl.when(at_top & at_side)
+    def _():
+        for copy in root_copies():
+            copy.start()
+        pltpu.make_async_copy(assembled.at[:, 0, low, wide], low_stage, recv0.at[0]).start()
+        pltpu.make_async_copy(assembled.at[0, :, high, wide], high_stage, recv0.at[1]).start()
+
+    @pl.when(at_top)
+    def _():
+        pltpu.make_async_copy(low_stage, low_stage, recv0.at[0]).wait()
+        for copy in low_copies():
+            copy.start()
+        pltpu.make_async_copy(low_stage.at[0], rows.at[0, x, low], recv1.at[0]).start()
+
+    @pl.when(at_side)
+    def _():
+        pltpu.make_async_copy(high_stage, high_stage, recv0.at[1]).wait()
+        for copy in high_copies():
+            copy.start()
+        pltpu.make_async_copy(high_stage.at[0], rows.at[y, 0, high], recv1.at[1]).start()
 
     def spread(part, targets, send, recv):
         copies = [
-            pltpu.make_async_remote_copy(
-                src_ref=part,
-                dst_ref=part,
-                send_sem=send.at[i],
-                recv_sem=recv.at[i],
-                device_id=device(to),
-                device_id_type=MESH,
-            )
-            for i, to in enumerate(targets)
+            remote(part, part, send.at[i], recv.at[i], device(to)) for i, to in enumerate(targets)
         ]
         for copy in copies:
             copy.start()
@@ -574,60 +658,80 @@
         for copy in copies:
             copy.wait()
 
+    mine_low, mine_high = rows.at[y, x, low], rows.at[y, x, high]
+    pltpu.make_async_copy(mine_low, mine_low, recv1.at[0]).wait()
+    a1 = spread(mine_low, line(me, "x"), send_x.at[0], recv_x.at[0])
+    pltpu.make_async_copy(mine_high, mine_high, recv1.at[1]).wait()
+    b1 = spread(mine_high, line(me, "y"), send_y.at[0], recv_y.at[0])
+    mine = rows.at[y, x]
+
     @pl.when(jnp.logical_not(stays))
     def _():
-        pltpu.make_async_remote_copy(
-            src_ref=mine,
-            dst_ref=columns.at[to_row],
-            send_sem=send1,
-            recv_sem=recv1,
-            device_id=(to_row, to_col),
-            device_id_type=MESH,
-        ).start()
+        remote(mine, columns.at[to_row], send2, recv2, (to_row, to_col)).start()
 
     @pl.when(stays)
     def _():
-        pltpu.make_async_copy(mine, columns.at[r], recv1).start()
-
-    a1 = spread(rows.at[y, x, low], line(me, "x"), send_x.at[0], recv_x.at[0])
-    b1 = spread(rows.at[y, x, high], line(me, "y"), send_y.at[0], recv_y.at[0])
-    held = columns.at[r]
-    pltpu.make_async_copy(held, held, recv1).wait()
-    z1 = spread(held, file(me), send_z, recv_z)
+        pltpu.make_async_copy(mine, columns.at[r], recv2).start()
+
     finish(a1)
     a2 = spread(rows.at[y, :, low], line(me, "y"), send_y.at[1], recv_y.at[1])
     finish(b1)
     b2 = spread(rows.at[:, x, high], line(me, "x"), send_x.at[1], recv_x.at[1])
+    held = columns.at[r]
+    pltpu.make_async_copy(held, held, recv2).wait()
+    z1 = spread(held, file(me), send_z, recv_z)
     finish(z1)
     finish(a2)
     finish(b2)
 
     @pl.when(jnp.logical_not(stays))
     def _():
-        pltpu.make_async_copy(mine, mine, send1).wait()
-
-    @pl.when(first)
-    def _():
-        whole = assembled.at[pl.ds(depth, 15 * depth), pl.ds(0, P_SIZE)]
-        pltpu.make_async_copy(whole, whole, send0).wait()
+        pltpu.make_async_copy(mine, mine, send2).wait()
+
+    @pl.when(at_top & at_side)
+    def _():
+        for copy in root_copies():
+            copy.wait_send()
+
+    @pl.when(at_top)
+    def _():
+        for copy in low_copies():
+            copy.wait_send()
+
+    @pl.when(at_side)
+    def _():
+        for copy in high_copies():
+            copy.wait_send()
 
 
 def share_panel(assembled):
     depth = assembled.shape[0] // 16
+    half = depth // 2
     anywhere = pl.BlockSpec(memory_space=pl.ANY)
     dma = pltpu.SemaphoreType.DMA
+    shapes = ((4, 4, depth, P_SIZE), (8, depth, P_SIZE), (4, half, P_SIZE), (4, depth - half, P_SIZE))
     return pl.pallas_call(
         panel_kernel,
-        out_shape=[
-            jax.ShapeDtypeStruct((4, 4, depth, P_SIZE), jnp.float32),
-            jax.ShapeDtypeStruct((8, depth, P_SIZE), jnp.float32),
+        out_shape=[jax.ShapeDtypeStruct(shape, jnp.float32) for shape in shapes],
+        in_specs=[anywhere],
+        out_specs=[anywhere] * 4,
+        scratch_shapes=[
+            dma((2, 3)),
+            dma((2,)),
+            dma((2, 3)),
+            dma((2,)),
+            dma,
+            dma,
+            dma((2, 3)),
+            dma((2, 3)),
+            dma((2, 3)),
+            dma((2, 3)),
+            dma((7,)),
+            dma((7,)),
         ],
-        in_specs=[anywhere],
-        out_specs=[anywhere] * 2,
-        scratch_shapes=[dma, dma, dma, dma, dma((2, 3)), dma((2, 3)), dma((2, 3)), dma((2, 3)), dma((7,)), dma((7,))],
         compiler_params=pltpu.CompilerParams(collective_id=3, has_side_effects=True),
         name="share_panel",
-    )(assembled)
+    )(assembled.reshape(4, 4, depth, assembled.shape[1]))[:2]
 
 
 def factor_blocks(work, inverse, first, last):
@@ -754,14 +858,14 @@
             pltpu.VMEM((width, P_SIZE), bf16),
             pltpu.VMEM((width, P_SIZE), bf16),
         ],
-        compiler_params=pltpu.CompilerParams(vmem_limit_bytes=48 << 20),
+        compiler_params=pltpu.CompilerParams(vmem_limit_bytes=62 << 20),
         name="update",
     )(place, rows_raw, columns_raw, inverse, factor, assembled)
 
 
 def local(front_matrix, child_tiles, owner_index, slot_index):
-    where, prev, last = routing(owner_index, slot_index)
-    assembled, inverse, factor = exchange(where, prev, last, child_tiles, front_matrix)
+    where, own = routing(owner_index, slot_index)
+    assembled, inverse, factor = exchange(where, own, child_tiles, front_matrix)
     rows, columns = share_panel(assembled)
     rows_loc, cols_loc = front_matrix.shape
     place = jnp.stack([lax.axis_index("row") * rows_loc, lax.axis_index("col") * cols_loc])

time: 446 us -> 430 us (0.964)
  Pallas kernels: 433 us -> 422 us
  local copies, waits for them, and re-layouts: 6.32 us -> 0.6 us
    pallas_call x2 -> x1, Pallas kernels: 99.8 us -> 73.7 us  [share_panel(): pl.pallas_call(panel_kernel, out_shape=[jax.ShapeDtypeStruct(shape, jnp.f...]
    pallas_call x1, Pallas kernels: 319 us -> 333 us  [exchange(): pl.pallas_call(exchange_kernel, out_shape=outs, in_specs=[pl.BlockSpec(me...]
where the time goes in v3:
time: 430 us; the launch traced here: 425 us
  Pallas kernels  422 us (98%)
    pallas_call x1, Pallas kernels, exchange(): pl.pallas_call(exchange_kernel, out_shape=outs, in_specs=[pl.BlockSpec(me...  333 us
    pallas_call x1, Pallas kernels, share_panel(): pl.pallas_call(panel_kernel, out_shape=[jax.ShapeDtypeStruct(shape, jnp.f...  73.7 us
    pallas_call x1, Pallas kernels, update(): pl.pallas_call(update_kernel, grid=(rows // tile,), out_shape=jax.ShapeDt...  15 us

profile of v3, /device:TPU:0, one launch (start us, length us, event | category | flops | bytes accessed | tf_op | source)
XLA Modules:
  0.0 425.3 jit_solution(9759973011167888273)
XLA Ops:
  0.0 0.9 convert_reduce_fusion
  0.9 0.7 multiply_add_fusion
  1.6 0.7 select_reduce_fusion
  2.3 0.6 concatenate.3.own_ref
  2.9 333.2 %exchange.1 = (f32[1536,768]{1,0:T(8,128)}, f32[4,4,16,88,128]{4,3,2,1,0:T(8,128)}, f32[4,4,16,88,128]{4,3,2,1,0:T(8,128)}, f32[4,4,16,80,128]{4,3,2,1,0:T(8,128...) custom-call(s32[256]{0:T(256)} %get-tuple-element.16.where_ref, ...), custom_call_target="tpu_custom_call" | custom-call | tf_op jit(solution)/shard_map/exchange/pallas_call | solution.py:500
  336.1 73.7 %share_panel.1 = (f32[4,4,96,512]{3,2,1,0:T(8,128)}, f32[8,96,512]{2,1,0:T(8,128)}, f32[4,48,512]{2,1,0:T(8,128)}, f32[4,48,512]{2,1,0:T(8,128)}) custom-call(f32[4,4,96,768]{3,2,1,0:T(8,128)} %bitcast.7), custom_call_target="tpu_custom_call" | custom-call | tf_op jit(solution)/shard_map/share_panel/pallas_call | solution.py:713
  409.8 0.6 pad_add_fusion.place
  410.4 15.0 %update.1 = f32[1536,768]{1,0:T(8,128)} custom-call(s32[2]{0:T(128)} %pad_add_fusion.place, f32[1536,512]{1,0:T(8,128)} %bitcast.8, f32[768,512]{1,0:T(8,128)} %bitcast.9, f32[512,512]{1,0:T(8,128)} %get-tuple-element.13.inverse, f32[512,512]{1,0:T(8,128)} %get-tuple-element.14.factor, f32[1536,768]{1,0:T(8,128)} %get-tuple-element.10.assembled), custom_call_target="tpu_custom_call" | custom-call | tf_op jit(solution)/shard_map/update/pallas_call | solution.py:842
  (1 shorter events, 0.0 us)

commit v4 on v3

--- a/solution.py
+++ b/solution.py
@@ -9,8 +9,8 @@
 
 P_SIZE = 512
 MESH = pl.DeviceIdType.MESH
-ROWS = (88, 88, 80)
-STARTS = (0, 88, 176)
+ROWS = (88, 80, 88)
+STARTS = (0, 88, 168)
 HALF = (40, 40, 40)
 ORDERS = ("zxy", "xyz", "yzx")
 SHIFTS = (2, 1, 3, 0)

time: 430 us -> 421 us (0.979)
  Pallas kernels: 422 us -> 416 us
    pallas_call x1, Pallas kernels: 333 us -> 328 us  [exchange(): pl.pallas_call(exchange_kernel, out_shape=outs, in_specs=[pl.BlockSpec(me...]
where the time goes in v4:
time: 421 us; the launch traced here: 419 us
  Pallas kernels  416 us (99%)
    pallas_call x1, Pallas kernels, exchange(): pl.pallas_call(exchange_kernel, out_shape=outs, in_specs=[pl.BlockSpec(me...  328 us
    pallas_call x1, Pallas kernels, share_panel(): pl.pallas_call(panel_kernel, out_shape=[jax.ShapeDtypeStruct(shape, jnp.f...  73.4 us
    pallas_call x1, Pallas kernels, update(): pl.pallas_call(update_kernel, grid=(rows // tile,), out_shape=jax.ShapeDt...  15 us

profile of v4, /device:TPU:0, one launch (start us, length us, event | category | flops | bytes accessed | tf_op | source)
XLA Modules:
  0.0 419.4 jit_solution(12400463029262820740)
XLA Ops:
  0.0 0.9 convert_reduce_fusion
  0.9 0.7 multiply_add_fusion
  1.6 0.7 select_reduce_fusion
  2.3 0.6 concatenate.3.own_ref
  2.9 327.5 %exchange.1 = (f32[1536,768]{1,0:T(8,128)}, f32[4,4,16,88,128]{4,3,2,1,0:T(8,128)}, f32[4,4,16,80,128]{4,3,2,1,0:T(8,128)}, f32[4,4,16,88,128]{4,3,2,1,0:T(8,128...) custom-call(s32[256]{0:T(256)} %get-tuple-element.16.where_ref, ...), custom_call_target="tpu_custom_call" | custom-call | tf_op jit(solution)/shard_map/exchange/pallas_call | solution.py:500
  330.4 73.4 %share_panel.1 = (f32[4,4,96,512]{3,2,1,0:T(8,128)}, f32[8,96,512]{2,1,0:T(8,128)}, f32[4,48,512]{2,1,0:T(8,128)}, f32[4,48,512]{2,1,0:T(8,128)}) custom-call(f32[4,4,96,768]{3,2,1,0:T(8,128)} %bitcast.7), custom_call_target="tpu_custom_call" | custom-call | tf_op jit(solution)/shard_map/share_panel/pallas_call | solution.py:713
  403.8 0.6 pad_add_fusion.place
  404.4 15.0 %update.1 = f32[1536,768]{1,0:T(8,128)} custom-call(s32[2]{0:T(128)} %pad_add_fusion.place, f32[1536,512]{1,0:T(8,128)} %bitcast.8, f32[768,512]{1,0:T(8,128)} %bitcast.9, f32[512,512]{1,0:T(8,128)} %get-tuple-element.13.inverse, f32[512,512]{1,0:T(8,128)} %get-tuple-element.14.factor, f32[1536,768]{1,0:T(8,128)} %get-tuple-element.10.assembled), custom_call_target="tpu_custom_call" | custom-call | tf_op jit(solution)/shard_map/update/pallas_call | solution.py:842
  (1 shorter events, 0.0 us)
